TPU v7x, 32 devices: a whole 2x2x4 slice. The times are simulated.
32 devices in a mesh: groups: 2 (over x), tensor: 16 (over z, y, core).
Axes of the slice: x: 2, y: 2, z: 4, core: 2. Of those that a mesh axis runs over, the one named last changes fastest.
Arguments:
- tokens: bfloat16 [24576, 8192], P(('groups', 'tensor')), parts along dimension 0, may hold values from -6 to 6
- norm_gain: float32 [8192], replicated, may hold values from 0.25 to 1.75
- w_kv: bfloat16 [8192, 1024], P('tensor'), may hold values from -0.0625 to 0.0625
- w_out: bfloat16 [4096, 8192], P(None, 'tensor'), may hold values from -0.09375 to 0.09375
- lengths: int32 [48], P('groups'), parts along dimension 0, may hold values from 1 to 512, 7680 in all
- request_owner: int32 [48], P('groups'), parts along dimension 0, may hold values from 0 to 15, as said below
- block_table: int32 [192], P('groups'), parts along dimension 0, may hold values from 0 to 95, as said below
- dec_query: bfloat16 [64, 4, 4096], P(('groups', 'tensor')), parts along dimension 0, may hold values from -400 to 400
- dec_new: bfloat16 [64, 4, 1024], P(('groups', 'tensor')), parts along dimension 0, may hold values from -5 to 5
Outputs:
- decoded: bfloat16 [64, 4, 8192], P('groups', None, 'tensor'), parts along dimension 0
There are 2 independent parts, one for each index of `groups`. A program takes and returns all parts, laid end to end along the dimension named above; an argument that names none is the same for every part. Nothing has to cross between parts.
Inputs may be any that keep to these rules, and one draw needn't show every extreme that they name: `request_owner`: no index of tensor owns more than 2 requests, and one owns exactly 2. block_table[r * 4 + j] is the pool block that holds positions j * 128 to (j + 1) * 128 - 1 of request r; every pool block appears once; the 6 pool blocks d * 6 to (d + 1) * 6 - 1 of one index d of tensor hold at most one block of the requests of any one owner.
All inputs are finite; a program needn't handle non-finite values.
Results may differ from a plain program's by a relative error of at most 0.0081.
Values may be sent and summed in bfloat16 or wider, within the bound.
No kernel may reach another device: no remote copies, remote signals or barrier semaphores. Data moves between devices by JAX's collectives and lax.ppermute only.
A program may use at most 128 MiB of HBM per device.

v0:
```python
import jax
import jax.numpy as jnp
from jax import lax
from jax.sharding import PartitionSpec as P

QH = 32
KVH = 4
HD = 128
BLK = 128
MAXBLK = 4
STEPS = 4
OWN_MAX = 2


norm_eps = 1e-05
masked_score = -1e30


def slot_tables(request_owner, lengths, block_table, slot_count):
    req_count = request_owner.shape[0]
    req_index = jnp.arange(req_count, dtype=jnp.int32)
    earlier = (request_owner[None, :] == request_owner[:, None]) & (
        req_index[None, :] < req_index[:, None]
    )
    owner_rank = jnp.sum(earlier.astype(jnp.int32), axis=1)
    slot_of = request_owner * OWN_MAX + owner_rank
    slot_hit = (slot_of[None, :] == jnp.arange(slot_count, dtype=jnp.int32)[:, None]).astype(
        jnp.int32
    )
    slot_live = jnp.sum(slot_hit, axis=1)
    slot_len = jnp.sum(slot_hit * lengths[None, :], axis=1)
    req_blocks = block_table.reshape(req_count, MAXBLK)
    source = jnp.sum(slot_hit[:, :, None] * req_blocks[None, :, :], axis=1)
    return (slot_live, source, slot_len)


def attend(dec_query, dec_new, cached, slot_len, slot_live):
    slot_rows = dec_query.shape[0]
    group = QH // KVH
    queries = dec_query.reshape(slot_rows, STEPS, KVH, group, HD)
    cache_keys = cached[:, 0]
    cache_values = cached[:, 1]
    new_keys = dec_new[:, :, : KVH * HD].reshape(slot_rows, STEPS, KVH, HD)
    new_values = dec_new[:, :, KVH * HD :].reshape(slot_rows, STEPS, KVH, HD)
    score_scale = HD ** (-0.5)
    past = (
        jnp.einsum("nikgd,nktd->nikgt", queries, cache_keys, preferred_element_type=jnp.float32)
        * score_scale
    )
    positions = jnp.arange(cache_keys.shape[2], dtype=jnp.int32)
    visible = positions[None, :] < slot_len[:, None]
    past = jnp.where(visible[:, None, None, None, :], past, masked_score)
    recent = (
        jnp.einsum("nikgd,njkd->nikgj", queries, new_keys, preferred_element_type=jnp.float32)
        * score_scale
    )
    step_index = jnp.arange(STEPS, dtype=jnp.int32)
    causal = step_index[None, :] <= step_index[:, None]
    recent = jnp.where(causal[None, :, None, None, :], recent, masked_score)
    highest = jnp.maximum(jnp.max(past, axis=-1), jnp.max(recent, axis=-1))
    past_exp = jnp.exp(past - highest[..., None])
    recent_exp = jnp.exp(recent - highest[..., None])
    total = jnp.sum(past_exp, axis=-1) + jnp.sum(recent_exp, axis=-1)
    past_probs = (past_exp / total[..., None]).astype(jnp.bfloat16)
    recent_probs = (recent_exp / total[..., None]).astype(jnp.bfloat16)
    mixed = jnp.einsum(
        "nikgt,nktd->nikgd", past_probs, cache_values, preferred_element_type=jnp.float32
    )
    mixed = mixed + jnp.einsum(
        "nikgj,njkd->nikgd", recent_probs, new_values, preferred_element_type=jnp.float32
    )
    mixed = mixed * slot_live.astype(jnp.float32)[:, None, None, None, None]
    return mixed.reshape(slot_rows, STEPS, QH * HD).astype(jnp.bfloat16)


def on_device(
    tokens, norm_gain, w_kv, w_out, lengths, request_owner, block_table, dec_query, dec_new
):
    axis_size = lax.axis_size("tensor")
    my_index = lax.axis_index("tensor")
    wide_tokens = tokens.astype(jnp.float32)
    inverse = lax.rsqrt(jnp.mean(wide_tokens * wide_tokens, axis=1, keepdims=True) + norm_eps)
    normed = (wide_tokens * inverse * norm_gain).astype(jnp.bfloat16)
    tok_rows = normed.shape[0]
    kv_width = w_kv.shape[1]
    kv_local = jnp.dot(
        normed,
        lax.all_gather(w_kv, "tensor", axis=0, tiled=True),
        preferred_element_type=jnp.float32,
    ).astype(jnp.bfloat16)
    slot_count = OWN_MAX * axis_size
    slot_live, source, slot_len = slot_tables(request_owner, lengths, block_table, slot_count)
    first_slot = my_index * OWN_MAX
    piece_width = kv_width // axis_size
    spread = (
        kv_local.reshape(tok_rows, axis_size, piece_width)
        .transpose(1, 0, 2)
        .reshape(axis_size, tok_rows * piece_width)
    )
    kv_pool = lax.all_to_all(spread, "tensor", split_axis=0, concat_axis=1, tiled=True).reshape(
        -1, BLK * piece_width
    )
    outgoing = kv_pool[source.reshape(-1)].reshape(
        axis_size, OWN_MAX * MAXBLK, 1, BLK * piece_width
    )
    incoming = lax.all_to_all(outgoing, "tensor", split_axis=0, concat_axis=2, tiled=True)
    head_parts = HD // piece_width
    cached = incoming.reshape(OWN_MAX, MAXBLK, 2, KVH, head_parts, BLK, piece_width)
    cached = cached.transpose(0, 2, 3, 1, 5, 4, 6).reshape(OWN_MAX, 2, KVH, MAXBLK * BLK, HD)
    my_live = lax.dynamic_slice_in_dim(slot_live, first_slot, OWN_MAX)
    my_len = lax.dynamic_slice_in_dim(slot_len, first_slot, OWN_MAX)
    attended = attend(dec_query, dec_new, cached, my_len, my_live)
    return jnp.einsum(
        "nsf,fo->nso",
        lax.all_gather(attended, "tensor", axis=0, tiled=True),
        w_out,
        preferred_element_type=jnp.float32,
    ).astype(jnp.bfloat16)


def solution(mesh):
    placed = (
        P(("groups", "tensor"), None),
        P(),
        P("tensor", None),
        P(None, "tensor"),
        P("groups"),
        P("groups"),
        P("groups"),
        P(("groups", "tensor"), None, None),
        P(("groups", "tensor"), None, None),
    )
    return jax.shard_map(
        on_device,
        mesh=mesh,
        in_specs=placed,
        out_specs=P("groups", None, "tensor"),
        check_vma=False,
    )
```

profile of v0, /device:TPU:0, one launch (start us, length us, event | category | flops | bytes accessed | tf_op | source)
XLA Modules:
  0.0 377.2 jit_solution(7746487110365468694)
XLA Ops:
  6.5 0.7 all-gather.3.cloned.1.call-update
  7.3 7.1 %fusion = f32[768]{0:T(1024)S(1)} fusion(bf16[768,8192]{1,0:T(8,128)(2,1)} %param.9), kind=kLoop, calls=%fused_computation.3 | loop fusion | flops 18873600 | bytes 12585984 | tf_op jit(solution)/shard_map/reduce_sum | solution.py:82
  14.4 124.8 %all-gather.3.cloned.1.call-done = bf16[8192,1024]{1,0:T(8,128)(2,1)} async-done(((bf16[512,1024]{1,0:T(8,128)(2,1)}), bf16[8192,1024]{1,0:T(8,128)(2,1)}) %all-gather.3.cloned.1.call-update) | async-done | bytes 16777232 | tf_op jit(solution)/shard_map/all_gather | solution.py:88
  139.1 0.0 copy-done.4
  139.1 18.3 %fusion.9 = bf16[768,1024]{1,0:T(8,128)(2,1)S(1)} fusion(bf16[8192,1024]{1,0:T(8,128)(2,1)} %all-gather.3.cloned.1.call-done, bf16[768,8192]{1,0:T(8,128)(2,1)} %param.9, f32[8192]{0:T(1024)S(1)} %copy-done.4, f32[768]{0:T(1024)S(1)} %add_rsqrt_fusion), kind=kOutput, calls=%fused_computation.11 | convolution fusion | flops 12910854144 | bytes 30968832 | tf_op jit(solution)/shard_map/dot_general | solution.py:86
  157.4 0.7 copy.50
  158.1 2.8 copy.51
  160.9 5.4 %all_to_all.26 = bf16[16,1,49152]{2,1,0:T(2,128)(2,1)S(1)} reshape(bf16[16,768,64]{2,1,0:T(8,128)(2,1)} %copy.51) | data formatting | bytes 3145728 | tf_op jit(solution)/shard_map/all_to_all | solution.py:100
  166.3 0.5 broadcast.76
  166.9 11.4 %reduce.1 = bf16[16,49152]{1,0:T(8,128)(2,1)} reduce(bf16[16,1,49152]{2,1,0:T(2,128)(2,1)S(1)} %all_to_all.26, bf16[]{:T(256)} %broadcast.76), dimensions={1}, to_apply=%all_to_all.26.reduce_sub_computation | reduce | bytes 3145730 | tf_op jit(solution)/shard_map/all_to_all | solution.py:100
  178.2 3.3 reshape.163
  181.6 4.6 %all-to-all-start = ((bf16[16,2,24576]{2,1,0:T(2,128)(2,1)}), bf16[16,2,24576]{2,1,0:T(2,128)(2,1)}, u32[]{:S(2)}, u32[]{:S(2)}) async-start(bf16[16,2,24576]{2,1,0:T(2,128)(2,1)} %reshape.163), calls=%async_computation | async-start | bytes 3145728 | tf_op jit(solution)/shard_map/all_to_all | solution.py:100
  186.2 0.1 mul.79
  186.3 0.1 copy.53
  186.4 0.2 convert_reduce_fusion
  186.6 0.1 fusion.31
  186.6 0.1 multiply_reduce_fusion
  186.7 0.1 copy.54
  186.8 0.1 reshape.141
  187.0 31.2 %all-to-all-done = bf16[16,2,24576]{2,1,0:T(2,128)(2,1)} async-done(((bf16[16,2,24576]{2,1,0:T(2,128)(2,1)}), bf16[16,2,24576]{2,1,0:T(2,128)(2,1)}, u32[]{:S(2)}, u32[]{:S(2)}) %all-to-all-start) | async-done | bytes 1572896 | tf_op jit(solution)/shard_map/all_to_all | solution.py:100
  218.1 8.1 %reshape.164 = bf16[16,1,49152]{2,1,0:T(2,128)(2,1)S(1)} reshape(bf16[16,2,24576]{2,1,0:T(2,128)(2,1)} %all-to-all-done) | data formatting | bytes 3145728
  226.2 10.7 %reduce = bf16[16,49152]{1,0:T(8,128)(2,1)} reduce(bf16[16,1,49152]{2,1,0:T(2,128)(2,1)S(1)} %reshape.164, bf16[]{:T(256)} %constant.31), dimensions={1}, to_apply=%all_to_all.22.reduce_sub_computation | reduce | bytes 3145730 | tf_op jit(solution)/shard_map/all_to_all | solution.py:100
  237.0 3.2 reshape.140
  240.2 3.2 gather_fusion
  243.4 9.2 %all-to-all-start.1 = ((bf16[16,8,1,8192]{3,1,2,0:T(8,128)(2,1)}), bf16[16,8,1,8192]{3,1,2,0:T(8,128)(2,1)S(1)}, u32[]{:S(2)}, u32[]{:S(2)}) async-start(bf16[16,8,1,8192]{3,1,2,0:T(8,128)(2,1)} %bitcast.74), calls=%async_computation.1 | async-start | bytes 4194304 | tf_op jit(solution)/shard_map/all_to_all | solution.py:106
  252.6 0.0 all-gather.5.cloned.1.call-start
  252.7 0.1 reshape.145
  252.8 0.1 fusion.37
  252.9 0.1 dynamic_slice.6
  253.0 0.1 dynamic-slice_convert_fusion
  253.0 0.1 iota_compare_fusion.2
  253.1 0.4 fusion.40
  253.5 40.2 %all-to-all-done.1 = bf16[16,8,1,8192]{3,1,2,0:T(8,128)(2,1)S(1)} async-done(((bf16[16,8,1,8192]{3,1,2,0:T(8,128)(2,1)}), bf16[16,8,1,8192]{3,1,2,0:T(8,128)(2,1)S(1)}, u32[]{:S(2)}, u32[]{:S(2)}) %all-to-all-start.1) | async-done | bytes 2097184 | tf_op jit(solution)/shard_map/all_to_all | solution.py:106
  293.7 1.3 copy-done
  295.1 2.7 copy.56
  297.8 5.5 %reshape.143 = bf16[2,4,2,4,2,128,64]{6,5,4,3,2,1,0:T(8,128)(2,1)} reshape(bf16[1,8,16,1,8192]{4,2,1,3,0:T(8,128)(2,1)S(1)} %copy.56) | data formatting | bytes 4194304 | tf_op jit(solution)/shard_map/reshape | solution.py:108
  303.4 8.5 %copy.69 = bf16[2,2,4,4,128,2,64]{6,5,4,3,2,0,1:T(2,128)(2,1)} copy(bf16[2,2,4,4,128,2,64]{6,4,5,2,1,3,0:T(8,128)(2,1)} %bitcast.72) | data formatting | bytes 4194304 | tf_op jit(solution)/shard_map/reshape | solution.py:109
  311.9 6.8 %reshape.161 = bf16[2,2,4,512,128]{4,3,2,0,1:T(8,128)(2,1)S(1)} reshape(bf16[2,2,4,4,128,2,64]{6,5,4,3,2,0,1:T(2,128)(2,1)} %copy.69) | data formatting | bytes 4194304 | tf_op jit(solution)/shard_map/reshape | solution.py:109
  318.7 0.5 fusion.39
  319.2 0.1 fusion.28
  319.3 0.2 fusion.23
  319.6 0.2 convolution_bitcast_fusion.1
  319.8 0.3 fusion.19
  320.2 0.7 convert_element_type.46
  320.8 0.0 all-gather.5.cloned.1.call-update
  320.8 44.6 %all-gather.5.cloned.1.call-done = bf16[32,4,4096]{2,1,0:T(4,128)(2,1)} async-done(((bf16[2,4,4096]{2,1,0:T(4,128)(2,1)}), bf16[32,4,4096]{2,1,0:T(4,128)(2,1)}) %all-gather.5.cloned.1.call-update) | async-done | bytes 1048592 | tf_op jit(solution)/shard_map/all_gather | solution.py:115
  365.4 3.7 fusion.14
  369.1 0.8 copy.64
  (21 shorter events, 0.1 us)
Async XLA Ops:
  6.5 132.6 %all-gather.3.cloned.1.call-start = ((), (), s32[]{:S(2)}) async-start(), calls=%async_computation.2 | async-start | bytes 17825792 | tf_op jit(solution)/shard_map/all_gather | solution.py:88
  7.3 131.9 %copy-start.4 = (f32[8192]{0:T(1024)S(1)}, f32[8192]{0:T(1024)}, u32[]{:S(2)}) copy-start(f32[8192]{0:T(1024)} %param.10) | copy-start | bytes 98308
  178.2 8.0 %copy-start.2 = (s32[96]{0:T(128)S(1)}, s32[96]{0:T(128)}, u32[]{:S(2)}) copy-start(s32[96]{0:T(128)} %param.15) | copy-start | bytes 1156
  178.2 8.1 %copy-start.6 = (s32[24]{0:T(128)S(1)}, s32[24]{0:T(128)}, u32[]{:S(2)}) copy-start(s32[24]{0:T(128)} %param.14) | copy-start | bytes 292
  181.6 36.6 %all-to-all-start = ((bf16[16,2,24576]{2,1,0:T(2,128)(2,1)}), bf16[16,2,24576]{2,1,0:T(2,128)(2,1)}, u32[]{:S(2)}, u32[]{:S(2)}) async-start(bf16[16,2,24576]{2,1,0:T(2,128)(2,1)} %reshape.163), calls=%async_computation | async-start | bytes 3145728 | tf_op jit(solution)/shard_map/all_to_all | solution.py:100
  243.4 9.3 %copy-start.1 = (bf16[2,4,4096]{2,1,0:T(4,128)(2,1)S(1)}, bf16[2,4,4096]{2,1,0:T(4,128)(2,1)}, u32[]{:S(2)}) copy-start(bf16[2,4,4096]{2,1,0:T(4,128)(2,1)} %param.16) | copy-start | bytes 196612
  243.4 9.4 %copy-start.3 = (s32[24]{0:T(128)S(1)}, s32[24]{0:T(128)}, u32[]{:S(2)}) copy-start(s32[24]{0:T(128)} %param.13) | copy-start | bytes 292
  243.4 9.7 %copy-start.5 = (bf16[2,4,1024]{2,1,0:T(4,128)(2,1)S(1)}, bf16[2,4,1024]{2,1,0:T(4,128)(2,1)}, u32[]{:S(2)}) copy-start(bf16[2,4,1024]{2,1,0:T(4,128)(2,1)} %param.17) | copy-start | bytes 49156
  243.4 50.3 %all-to-all-start.1 = ((bf16[16,8,1,8192]{3,1,2,0:T(8,128)(2,1)}), bf16[16,8,1,8192]{3,1,2,0:T(8,128)(2,1)S(1)}, u32[]{:S(2)}, u32[]{:S(2)}) async-start(bf16[16,8,1,8192]{3,1,2,0:T(8,128)(2,1)} %bitcast.74), calls=%async_computation.1 | async-start | bytes 4194304 | tf_op jit(solution)/shard_map/all_to_all | solution.py:106
  252.6 112.8 %all-gather.5.cloned.1.call-start = ((), (), s32[]{:S(2)}) async-start(), calls=%async_computation.3 | async-start | bytes 1114112 | tf_op jit(solution)/shard_map/all_gather | solution.py:115
  293.7 1.4 copy-start
Sparse Core Ops, SparseCore 0:
  9.5 129.5 all-gather.2
  320.9 44.4 all-gather.4
where the time goes:
time: 384 us; the launch traced here: 377 us
  waiting for transfers between devices  241 us (63%)
  local copies, waits for them, and re-layouts  54.2 us (14%)
  other arithmetic  30.2 us (8%)
  matrix products  23.5 us (6%)
  between operations  14 us (4%)
  starting transfers between devices  13.9 us (4%)
    all_gather x1, waiting for transfers between devices, on_device(): lax.all_gather(w_kv, 'tensor', axis=0, tiled=True)  125 us
    all_gather x1, waiting for transfers between devices, on_device(): lax.all_gather(attended, 'tensor', axis=0, tiled=True)  44.6 us
    all_to_all x1, waiting for transfers between devices, on_device(): lax.all_to_all(outgoing, 'tensor', split_axis=0, concat_axis=2, tiled=True)  40.2 us
    all_to_all x1, waiting for transfers between devices, on_device(): lax.all_to_all(spread, 'tensor', split_axis=0, concat_axis=1, tiled=True)  31.2 us
    all_to_all x2, other arithmetic, on_device(): lax.all_to_all(spread, 'tensor', split_axis=0, concat_axis=1, tiled=True)  22.1 us
    dot_general x1, matrix products, on_device(): jnp.dot(normed, lax.all_gather(w_kv, 'tensor', axis=0, tiled=True), prefe...  18.3 us
    reshape x2, local copies, waits for them, and re-layouts, on_device(): cached.transpose(0, 2, 3, 1, 5, 4, 6)  15.3 us
    unnamed x16, local copies, waits for them, and re-layouts  12.8 us
  transfers between devices with their start and end apart: 4, of which 4 were waited for; matrix products, arithmetic and copies ran while one was open for 2% of the time, Pallas kernels for 0%

commit v1 on v0

v1 whole, which is shorter than its diff:
```python
import functools

import jax
import jax.numpy as jnp
from jax import lax
from jax.experimental import pallas as pl
from jax.experimental.pallas import tpu as pltpu
from jax.sharding import PartitionSpec as P

QH = 32
KVH = 4
HD = 128
BLK = 128
MAXBLK = 4
STEPS = 4
OWN_MAX = 2
CORES = 2
LOCAL_KV = KVH // CORES
GROUP = QH // KVH
ROWS = GROUP * STEPS
LOCAL_ROWS = LOCAL_KV * ROWS
OWN_ROWS = 2 * LOCAL_KV * STEPS
QROWS = LOCAL_ROWS + OWN_ROWS
STAT_ROWS = 16

norm_eps = 1e-05
masked_score = -1e30
VMEM_LIMIT = 48 * 1024 * 1024


class Links:
    def __init__(self, groups, tensor):
        self.groups, self.tensor = groups, tensor
        self.nz = tensor // 4

    def move(self, value, kind, hops=1):
        pairs = []
        for g in range(self.groups):
            for t in range(self.tensor):
                to_g, to_t = g, t
                if kind == "c":
                    to_t = t ^ 1
                elif kind == "y":
                    to_t = t ^ 2
                elif kind == "yc":
                    to_t = t ^ 3
                elif kind == "z":
                    to_t = (t + 4 * hops) % self.tensor
                else:
                    to_g = g ^ 1
                pairs.append((g * self.tensor + t, to_g * self.tensor + to_t))
        return lax.ppermute(value, ("groups", "tensor"), pairs)


def tied(value, others):
    if not others:
        return value
    return lax.optimization_barrier((value,) + tuple(others))[0]


def split_columns(w_kv, core, half):
    rows, width = w_kv.shape
    part = width // (2 * CORES)
    gran = rows // 2

    def kernel(core_ref, half_ref, a, b, c, d, out_a, out_b, out_c, out_d):
        for src, dst in ((a, out_a), (b, out_b), (c, out_c), (d, out_d)):
            dst[...] = src[...]

    whole, halved = pl.BlockSpec((rows, part), lambda j, c, h: (0, j)), pl.BlockSpec(
        (gran, part), lambda j, c, h: (0, j)
    )
    return pl.pallas_call(
        kernel,
        grid_spec=pltpu.PrefetchScalarGridSpec(
            num_scalar_prefetch=2,
            grid=(2,),
            in_specs=[
                pl.BlockSpec((rows, part), lambda j, c, h: (0, CORES * j + c[0])),
                pl.BlockSpec((rows, part), lambda j, c, h: (0, CORES * j + 1 - c[0])),
                pl.BlockSpec((gran, part), lambda j, c, h: (h[0], CORES * j + c[0])),
                pl.BlockSpec((gran, part), lambda j, c, h: (h[0], CORES * j + 1 - c[0])),
            ],
            out_specs=[whole, whole, halved, halved],
        ),
        out_shape=[
            jax.ShapeDtypeStruct((n, 2 * part), w_kv.dtype) for n in (rows, rows, gran, gran)
        ],
        name="split",
    )(core.reshape(1), half.reshape(1), w_kv, w_kv, w_kv, w_kv)


def scale_kernel(chunk, tok_ref, out_ref):
    width = tok_ref.shape[1]
    acc = None
    for c in range(0, width, chunk):
        wide = tok_ref[:, c : c + chunk].astype(jnp.float32)
        acc = wide * wide if acc is None else acc + wide * wide
    inverse = lax.rsqrt(jnp.sum(acc, axis=1, keepdims=True) / width + norm_eps)
    out_ref[...] = jnp.broadcast_to(inverse, out_ref.shape)


def row_scale(tokens):
    rows, width = tokens.shape
    tile = 128
    return pl.pallas_call(
        functools.partial(scale_kernel, 512),
        grid=(rows // tile,),
        in_specs=[pl.BlockSpec((tile, width), lambda i: (i, 0))],
        out_specs=pl.BlockSpec((tile, 128), lambda i: (i, 0)),
        out_shape=jax.ShapeDtypeStruct((rows, 128), jnp.float32),
        compiler_params=pltpu.CompilerParams(vmem_limit_bytes=VMEM_LIMIT),
        cost_estimate=pl.CostEstimate(
            flops=2 * rows * width, bytes_accessed=2 * rows * width, transcendentals=rows
        ),
        name="row_scale",
    )(tokens)


def partial_sum(acc, lhs, scale_ref, gains, pieces, granules):
    scale = scale_ref[:, :1]
    at = 0
    for ref, count in zip(pieces, granules):
        size = ref.shape[0] // count
        for j in range(count):
            wide = lhs[at][...].astype(jnp.float32)
            normed = (wide * scale * gains[at][...]).astype(jnp.bfloat16)
            term = jnp.dot(
                normed, ref[j * size : (j + 1) * size, :], preferred_element_type=jnp.float32
            )
            acc = term if acc is None else acc + term
            at += 1
    return acc


def project_kernel(has_acc, granules, tiles, offs_ref, *refs):
    n = sum(granules)
    lead = 1 if has_acc else 0
    own, other = refs[lead : lead + n], refs[lead + n : lead + 2 * n]
    gains = refs[lead + 2 * n : lead + 3 * n]
    own_scale, other_scale = refs[lead + 3 * n : lead + 3 * n + 2]
    pieces, out_ref = refs[lead + 3 * n + 2 : -1], refs[-1]
    i = pl.program_id(0)

    def run(lhs, scale_ref):
        acc = refs[0][...] if has_acc else None
        out_ref[...] = partial_sum(acc, lhs, scale_ref, gains, pieces, granules)

    @pl.when(i < tiles)
    def _():
        run(own, own_scale)

    @pl.when(i >= tiles)
    def _():
        run(other, other_scale)


def token_specs(tile, tiles, gran, n):
    def own_row(i):
        return jnp.minimum(i, tiles - 1)

    def other_row(i):
        return jnp.maximum(i - tiles, 0)

    specs = []
    for row in (own_row, other_row):
        for j in range(n):
            specs.append(
                pl.BlockSpec((tile, gran), lambda i, s, *_, j=j, row=row: (row(i), s[j]))
            )
    for j in range(n):
        specs.append(pl.BlockSpec((1, gran), lambda i, s, *_, j=j: (0, s[j])))
    for row in (own_row, other_row):
        specs.append(pl.BlockSpec((tile, 128), lambda i, s, *_, row=row: (row(i), 0)))
    return specs


def project(acc, tok, pieces, gran):
    own, other, gain, own_scale, other_scale = tok
    rows, width = own.shape
    cols = pieces[0][0].shape[1]
    tile = 384
    tiles = rows // tile
    granules = [len(o) for _, o in pieces]
    n = sum(granules)
    offs = jnp.stack([o for _, os in pieces for o in os]).astype(jnp.int32)
    acc_spec = pl.BlockSpec((tile, cols), lambda i, s: (i, 0))
    in_specs = ([acc_spec] if acc is not None else []) + token_specs(tile, tiles, gran, n)
    for a, _ in pieces:
        in_specs.append(pl.BlockSpec(a.shape, lambda i, s: (0, 0)))
    args = ([acc] if acc is not None else []) + [own] * n + [other] * n + [gain] * n
    args += [own_scale, other_scale] + [a for a, _ in pieces]
    return pl.pallas_call(
        functools.partial(project_kernel, acc is not None, granules, tiles),
        grid_spec=pltpu.PrefetchScalarGridSpec(
            num_scalar_prefetch=1, grid=(2 * tiles,), in_specs=in_specs, out_specs=acc_spec
        ),
        out_shape=jax.ShapeDtypeStruct((2 * rows, cols), jnp.float32),
        compiler_params=pltpu.CompilerParams(vmem_limit_bytes=VMEM_LIMIT),
        cost_estimate=pl.CostEstimate(
            flops=4 * rows * n * gran * cols, bytes_accessed=8 * rows * cols, transcendentals=0
        ),
        name="project",
    )(offs, *args)


def attend_block(keys, values, query, fresh, fresh_values, head, visible, first):
    scale = HD**-0.5
    dims = (((1,), (1,)), ((), ()))
    past = lax.dot_general(query, keys, dims, preferred_element_type=jnp.float32) * scale
    recent = lax.dot_general(query, fresh, dims, preferred_element_type=jnp.float32) * scale
    where = lax.broadcasted_iota(jnp.int32, past.shape, 1)
    past = jnp.where(where < visible, past, masked_score)
    col = lax.broadcasted_iota(jnp.int32, recent.shape, 1) - head * STEPS
    step = lax.broadcasted_iota(jnp.int32, recent.shape, 0) % STEPS
    recent = jnp.where((col >= 0) & (col <= step) & (first > 0), recent, masked_score)
    top = jnp.maximum(
        jnp.max(past, axis=1, keepdims=True), jnp.max(recent, axis=1, keepdims=True)
    )
    past = jnp.exp(past - top)
    recent = jnp.exp(recent - top)
    total = jnp.sum(past, axis=1, keepdims=True) + jnp.sum(recent, axis=1, keepdims=True)
    out = jnp.dot(past.astype(jnp.bfloat16), values, preferred_element_type=jnp.float32)
    out = out + jnp.dot(
        recent.astype(jnp.bfloat16), fresh_values, preferred_element_type=jnp.float32
    )
    return out / total, top + jnp.log(total)


def as_row(column):
    n = column.shape[0]
    eye = lax.broadcasted_iota(jnp.int32, (n, n), 0) == lax.broadcasted_iota(jnp.int32, (n, n), 1)
    return jnp.sum(jnp.where(eye, column, 0.0), axis=0, keepdims=True)


def attend_half(kv, base, table_ref, q_ref, out_ref, blocks):
    stats = []
    for b in range(blocks):
        slot = table_ref[base + b, 0]
        visible = table_ref[base + b, 1]
        first = table_ref[base + b, 2]
        q = q_ref[slot]
        fresh = q[LOCAL_ROWS:]
        turned = jnp.concatenate([fresh[OWN_ROWS // 2 :], fresh[: OWN_ROWS // 2]], axis=0)
        block = kv[b * BLK : (b + 1) * BLK]
        lses = []
        for h in range(LOCAL_KV):
            keys = block[:, h * HD : (h + 1) * HD]
            values = block[:, (LOCAL_KV + h) * HD : (LOCAL_KV + h + 1) * HD]
            query = q[h * ROWS : (h + 1) * ROWS]
            out, lse = attend_block(keys, values, query, fresh, turned, h, visible, first)
            at = b * LOCAL_ROWS + h * ROWS
            out_ref[0, at : at + ROWS, :] = out.astype(jnp.bfloat16)
            lses.append(lse)
        lse = as_row(jnp.concatenate(lses, axis=0))
        high = lse.astype(jnp.bfloat16).astype(jnp.float32)
        mid = (lse - high).astype(jnp.bfloat16).astype(jnp.float32)
        low = lse - high - mid
        stats.append(jnp.concatenate([high, mid], axis=1))
        stats.append(jnp.concatenate([low, jnp.zeros_like(low)], axis=1))
    stats.append(jnp.zeros((STAT_ROWS - 2 * blocks, 2 * LOCAL_ROWS), jnp.float32))
    at = blocks * LOCAL_ROWS
    out_ref[0, at : at + STAT_ROWS, :] = jnp.concatenate(stats, axis=0).astype(jnp.bfloat16)


def attend_kernel(granules, blocks, offs_ref, table_ref, *refs):
    n = sum(granules)
    acc, own, other, gains = refs[0], refs[1 : 1 + n], refs[1 + n : 1 + 2 * n], refs[1 + 2 * n : 1 + 3 * n]
    own_scale, other_scale = refs[1 + 3 * n : 3 + 3 * n]
    pieces, q_ref, out_ref = refs[3 + 3 * n : -2], refs[-2], refs[-1]
    i = pl.program_id(0)

    def run(lhs, scale_ref, base):
        kv = partial_sum(acc[...], lhs, scale_ref, gains, pieces, granules).astype(jnp.bfloat16)
        attend_half(kv, base, table_ref, q_ref, out_ref, blocks)

    @pl.when(i == 0)
    def _():
        run(own, own_scale, 0)

    @pl.when(i == 1)
    def _():
        run(other, other_scale, blocks)


def attend(acc, tok, pieces, gran, table, queries):
    own, other, gain, own_scale, other_scale = tok
    rows, width = own.shape
    cols = acc.shape[1]
    blocks = rows // BLK
    granules = [len(o) for _, o in pieces]
    n = sum(granules)
    offs = jnp.stack([o for _, os in pieces for o in os]).astype(jnp.int32)
    in_specs = [pl.BlockSpec((rows, cols), lambda i, s, t: (i, 0))]
    in_specs += token_specs(rows, 1, gran, n)
    for a, _ in pieces:
        in_specs.append(pl.BlockSpec(a.shape, lambda i, s, t: (0, 0)))
    in_specs.append(pl.BlockSpec(queries.shape, lambda i, s, t: (0, 0, 0)))
    out_rows = blocks * LOCAL_ROWS + STAT_ROWS
    args = [acc] + [own] * n + [other] * n + [gain] * n + [own_scale, other_scale]
    args += [a for a, _ in pieces] + [queries]
    return pl.pallas_call(
        functools.partial(attend_kernel, granules, blocks),
        grid_spec=pltpu.PrefetchScalarGridSpec(
            num_scalar_prefetch=2,
            grid=(2,),
            in_specs=in_specs,
            out_specs=pl.BlockSpec((1, out_rows, HD), lambda i, s, t: (i, 0, 0)),
        ),
        out_shape=jax.ShapeDtypeStruct((2, out_rows, HD), jnp.bfloat16),
        compiler_params=pltpu.CompilerParams(vmem_limit_bytes=VMEM_LIMIT),
        cost_estimate=pl.CostEstimate(
            flops=4 * rows * n * gran * cols, bytes_accessed=8 * rows * cols, transcendentals=0
        ),
        name="attend",
    )(offs, table, *args)


def combine_kernel(halves, blocks, slots, slot_ref, slot_row_ref, *refs):
    ins, out_ref, acc_ref = refs[:-2], refs[-2], refs[-1]
    acc_ref[...] = jnp.zeros_like(acc_ref)
    per = 8
    rows = []
    for a, j in halves:
        stat = ins[a][j, blocks * LOCAL_ROWS :, :].astype(jnp.float32)
        for b in range(blocks):
            high, low = stat[2 * b : 2 * b + 1], stat[2 * b + 1 : 2 * b + 2]
            rows.append(high[:, :LOCAL_ROWS] + high[:, LOCAL_ROWS:] + low[:, :LOCAL_ROWS])
        rows.append(jnp.full((per - blocks, LOCAL_ROWS), masked_score, jnp.float32))
    lse = jnp.concatenate(rows, axis=0)
    lse = jnp.concatenate([lse, jnp.zeros_like(lse)], axis=1)
    lse = jnp.concatenate(
        [lse[k : k + 128].T[:LOCAL_ROWS] for k in range(0, lse.shape[0], 128)], axis=1
    )
    owner = slot_row_ref[...]
    weight = jnp.zeros_like(lse)
    for s in range(slots):
        mine = owner == s
        here = jnp.where(mine, lse, 2 * masked_score)
        top = jnp.max(here, axis=1, keepdims=True)
        grown = jnp.where(mine, jnp.exp(here - top), 0.0)
        total = jnp.sum(grown, axis=1, keepdims=True)
        weight = jnp.where(mine, grown / jnp.maximum(total, 1e-30), weight)
    for e, (a, j) in enumerate(halves):
        for b in range(blocks):
            at = e * per + b
            slot = slot_ref[at]
            part = ins[a][j, b * LOCAL_ROWS : (b + 1) * LOCAL_ROWS, :].astype(jnp.float32)
            acc_ref[slot] = acc_ref[slot] + part * weight[:, at : at + 1]
    for s in range(slots):
        value = acc_ref[s].reshape(LOCAL_ROWS // STEPS, STEPS, HD)
        if s % 4 == 0:
            held = []
        held.append(value)
        if s % 4 == 3:
            out_ref[:, (s - 3) * STEPS : (s + 1) * STEPS, :] = jnp.concatenate(
                held, axis=1
            ).astype(jnp.bfloat16)


def combine(parts, halves, blocks, slots, entry_slots):
    heads = LOCAL_ROWS // STEPS
    entries = entry_slots.shape[0]
    return pl.pallas_call(
        functools.partial(combine_kernel, halves, blocks, slots),
        in_specs=[
            pl.BlockSpec(memory_space=pltpu.SMEM),
            pl.BlockSpec(memory_space=pltpu.VMEM),
        ]
        + [pl.BlockSpec(memory_space=pltpu.VMEM) for _ in parts],
        out_specs=pl.BlockSpec(memory_space=pltpu.VMEM),
        out_shape=jax.ShapeDtypeStruct((heads, slots * STEPS, HD), jnp.bfloat16),
        scratch_shapes=[pltpu.VMEM((slots, LOCAL_ROWS, HD), jnp.float32)],
        compiler_params=pltpu.CompilerParams(vmem_limit_bytes=VMEM_LIMIT),
        name="combine",
    )(entry_slots, entry_slots.reshape(1, entries), *parts)


def out_kernel(has_acc, which_ref, x_ref, w_ref, *refs):
    acc = refs[0][...] if has_acc else None
    for h in range(x_ref.shape[0]):
        term = jnp.dot(
            x_ref[h], w_ref[h * HD : (h + 1) * HD, :], preferred_element_type=jnp.float32
        )
        acc = term if acc is None else acc + term
    refs[-1][...] = acc.astype(refs[-1].dtype)


def out_project(x, w_out, half, acc, dtype):
    heads, rows, _ = x.shape
    cols = w_out.shape[1]
    in_specs = [
        pl.BlockSpec(x.shape, lambda i, s: (0, 0, 0)),
        pl.BlockSpec((heads * HD, cols), lambda i, s: (s[0], 0)),
    ]
    if acc is not None:
        in_specs.append(pl.BlockSpec((rows, cols), lambda i, s: (0, 0)))
    return pl.pallas_call(
        functools.partial(out_kernel, acc is not None),
        grid_spec=pltpu.PrefetchScalarGridSpec(
            num_scalar_prefetch=1,
            grid=(1,),
            in_specs=in_specs,
            out_specs=pl.BlockSpec((rows, cols), lambda i, s: (0, 0)),
        ),
        out_shape=jax.ShapeDtypeStruct((rows, cols), dtype),
        compiler_params=pltpu.CompilerParams(vmem_limit_bytes=VMEM_LIMIT),
        cost_estimate=pl.CostEstimate(
            flops=2 * rows * heads * HD * cols, bytes_accessed=2 * heads * HD * cols,
            transcendentals=0,
        ),
        name="out_project",
    )(half.reshape(1), x, w_out, *([acc] if acc is not None else []))


def block_tables(request_owner, lengths, block_table, n_blocks):
    req_count = request_owner.shape[0]
    req_index = jnp.arange(req_count, dtype=jnp.int32)
    earlier = (request_owner[None, :] == request_owner[:, None]) & (
        req_index[None, :] < req_index[:, None]
    )
    slot_of = request_owner * OWN_MAX + jnp.sum(earlier.astype(jnp.int32), axis=1)
    place = jnp.arange(n_blocks, dtype=jnp.int32) % MAXBLK
    slot = jnp.repeat(slot_of, MAXBLK)
    visible = jnp.clip(jnp.repeat(lengths, MAXBLK) - place * BLK, 0, BLK)
    hit = (block_table[None, :] == jnp.arange(n_blocks, dtype=jnp.int32)[:, None]).astype(jnp.int32)
    values = jnp.stack([slot, visible, (place == 0).astype(jnp.int32)], axis=0)
    return jnp.sum(hit[:, None, :] * values[None, :, :], axis=2)


ORDER = [
    "zB1", "yC", "qp", "c", "qc", "yB0", "zB2", "ex", "zq1", "xB1", "yq0", "pair", "zC1", "yBz1",
    "xC0", "stat", "zB3", "yBx1", "xB2", "inv", "yBz2", "zC2", "xC1", "yq1", "zq2", "xB3", "G1",
    "zC3", "yBz3", "xC2", "yBx2", "zq3", "G2", "xC3", "yq3", "yq2", "yBx3", "G3",
]
WAITS = {
    "ex": ["yC", "qc"], "xC0": ["zB2"], "stat": ["zq1"], "zB3": ["yB0", "xB1", "yq0"],
    "xB2": ["xC0"], "inv": ["yBz1"], "zq2": ["ex", "inv"], "xB3": ["yBx1"], "G1": ["xB2"],
    "zC3": ["yBz2", "xC1", "yq1"], "yBz3": ["zq2"], "zq3": ["xB3"], "xC3": ["yBz3"],
    "yq3": ["yBx2"], "yq2": ["xC2"],
}


def any_order(nz):
    order = ["zB1", "yC", "yB0", "c", "qp", "qc", "yq0", "ex", "stat", "inv", "pair", "xC0"]
    for k in range(1, nz):
        order += [f"xB{k}", f"zC{k}", f"yBz{k}", f"zq{k}"]
        order += [f"zB{k + 1}"] if k < nz - 1 else []
        order += [f"yBx{k}", f"xC{k}", f"yq{k}"]
        order += [f"G{k}"]
    return order


def on_device(
    links, tokens, norm_gain, w_kv, w_out, lengths, request_owner, block_table, dec_query, dec_new
):
    size, nz = links.tensor, links.nz
    me = lax.axis_index("tensor")
    half = lax.axis_index("groups") % 2
    core = me % CORES
    rows = w_kv.shape[0]
    gran = rows // 2
    blocks = tokens.shape[0] // BLK
    n_blocks = block_table.shape[0]
    slots = OWN_MAX * size
    h0, h1 = half, 1 - half

    mine, theirs, mine_half, theirs_half = split_columns(w_kv, core, half)
    got = {}

    def back(k):
        return (me + size - 4 * k) % size

    def queries_here():
        q = dec_query.reshape(OWN_MAX, STEPS, CORES, LOCAL_ROWS // STEPS, HD)
        q = q.transpose(2, 0, 3, 1, 4).reshape(CORES, OWN_MAX, LOCAL_ROWS, HD)
        new = dec_new.reshape(OWN_MAX, STEPS, 2, CORES, LOCAL_KV, HD).transpose(3, 0, 2, 4, 1, 5)
        return jnp.concatenate([q, new.reshape(CORES, OWN_MAX, OWN_ROWS, HD)], axis=2)

    def at(device, halved):
        return device * 2 + halved

    def piece(name):
        if name == "mine":
            return mine, [at(me, 0), at(me, 1)]
        if name == "c":
            return got[name], [at(me ^ 1, 0), at(me ^ 1, 1)]
        if name == "yB0":
            return got[name], [at(me ^ 2, 0), at(me ^ 2, 1)]
        if name == "yC":
            return got[name], [at(me ^ 3, h0)]
        if name == "xC0":
            return got[name], [at(me ^ 3, h1)]
        there = back(int(name[-1]))
        kind = name[:-1]
        where = {
            "zB": [at(there, h0)],
            "xB": [at(there, h1)],
            "yBz": [at(there ^ 2, h0)],
            "yBx": [at(there ^ 2, h1)],
            "zC": [at(there ^ 1, h0), at(there ^ 3, h0)],
            "xC": [at(there ^ 1, h1), at(there ^ 3, h1)],
        }[kind]
        return got[name], where

    def stage(i):
        if i == 1:
            names = ["mine", "c", "yB0", "zB1", "xB1", "yC", "xC0", "zC1"]
        else:
            k = i - 1
            names = [f"yBz{k}", f"yBx{k}", f"zB{k + 1}", f"xB{k + 1}", f"zC{k + 1}", f"xC{k}"]
        return names

    last = [f"yBz{nz - 1}", f"yBx{nz - 1}", f"xC{nz - 1}"]
    acc = None
    order = ORDER if nz == 4 else any_order(nz)
    for name in order:
        waits = [got[w] for w in WAITS.get(name, [])] if nz == 4 else []
        kind, k = name.rstrip("0123456789"), int(name[-1]) if name[-1].isdigit() else 0
        with jax.named_scope(name):
            if kind == "G":
                if k == nz - 1 or nz == 4 and k == 3:
                    names = stage(k)
                else:
                    names = stage(k)
                pieces = [piece(n) for n in names]
                pieces[-1] = (tied(pieces[-1][0], waits), pieces[-1][1])
                acc = project(acc, tok, pieces, gran)
                continue
            if kind == "stat":
                scales = row_scale(tied(tokens, waits))
                continue
            if kind == "qp":
                q = queries_here()
                q_mine = lax.dynamic_index_in_dim(q, core, 0, keepdims=False)
                q_other = lax.dynamic_index_in_dim(q, 1 - core, 0, keepdims=False)
                continue
            if kind == "pair":
                c_half = lax.dynamic_slice_in_dim(got["c"], half * gran, gran, 0)
                got["pair"] = jnp.concatenate([tied(c_half, waits), got["yC"]], 0)
                continue
            if kind == "zq" and k == 1:
                got["zq0"] = jnp.stack([q_mine, got["qc"]])
            sources = {
                "c": theirs,
                "ex": tokens,
                "inv": None if kind != "inv" else scales,
                "qc": None if kind != "qc" else q_other,
                "yC": theirs_half,
                "yB": mine,
                "zB": mine_half if k == 1 else got.get(f"zB{k - 1}"),
                "xB": got.get(f"zB{k}"),
                "yBz": got.get(f"zB{k}"),
                "yBx": got.get(f"xB{k}"),
                "zC": got.get("pair") if k == 1 else got.get(f"zC{k - 1}"),
                "xC": got.get(f"zC{k}") if k else got.get("yC"),
                "zq": got.get(f"zq{k - 1}"),
                "yq": got.get(f"zq{k}"),
            }
            if kind == "yq" and k == 0 and "zq0" not in got:
                got["zq0"] = jnp.stack([q_mine, got["qc"]])
                sources["yq"] = got["zq0"]
            along = {"c": "c", "ex": "c", "inv": "c", "qc": "c", "yC": "yc"}.get(kind, kind[0])
            got[name] = links.move(tied(sources[kind], waits), along)
        if kind == "inv":
            tok = (tokens, got["ex"], norm_gain.reshape(1, -1), scales, got["inv"])

    queries = jnp.stack(
        [jnp.stack([got[f"zq{k}"], got[f"yq{k}"]]) for k in range(nz)]
    ).reshape(slots, QROWS, HD)

    tables = block_tables(request_owner, lengths, block_table, n_blocks)
    chip = jnp.concatenate(
        [
            lax.dynamic_slice_in_dim(tables, me * blocks, blocks, 0),
            lax.dynamic_slice_in_dim(tables, (me ^ 1) * blocks, blocks, 0),
        ]
    )
    slot = chip[:, 0]
    holder = slot // OWN_MAX
    far = holder // CORES
    q_at = (me // 4 - far // 2) % nz * 2 + ((far ^ (me // CORES)) & 1)
    q_at = (q_at * CORES + ((holder ^ me) & 1)) * OWN_MAX + slot % OWN_MAX
    table = jnp.stack([q_at, chip[:, 1], chip[:, 2]], axis=1)
    outs = attend(acc, tok, [piece(n) for n in last], gran, table, queries)

    parts, entries = [], []

    def arrived(value, device):
        entries.extend([(len(parts), 0, device), (len(parts), 1, device ^ 1)])
        parts.append(value)

    arrived(outs, me)
    z_got = {}
    for k in range(1, nz):
        with jax.named_scope(f"oz{k}"):
            z_got[k] = links.move(outs, "z", k)
        arrived(z_got[k], back(k))
    for k in range(nz):
        with jax.named_scope(f"oy{k}"):
            arrived(links.move(z_got[k] if k else outs, "y"), back(k) ^ 2)
    devices = jnp.stack([d for _, _, d in entries])
    entry = jnp.take(tables[:, 0].reshape(size, blocks), devices, axis=0)
    entry = jnp.pad(entry, ((0, 0), (0, 8 - blocks)), constant_values=-1).reshape(-1)
    attended = combine(parts, [(a, j) for a, j, _ in entries], blocks, slots, entry)
    with jax.named_scope("swap_attended"):
        attended_other = links.move(attended, "c")
    total = out_project(attended, w_out, core, None, jnp.float32)
    out = out_project(attended_other, w_out, 1 - core, total, jnp.bfloat16)
    return out.reshape(slots, STEPS, w_out.shape[1])


def solution(mesh):
    placed = (
        P(("groups", "tensor"), None),
        P(),
        P("tensor", None),
        P(None, "tensor"),
        P("groups"),
        P("groups"),
        P("groups"),
        P(("groups", "tensor"), None, None),
        P(("groups", "tensor"), None, None),
    )
    links = Links(mesh.shape["groups"], mesh.shape["tensor"])
    return jax.shard_map(
        functools.partial(on_device, links),
        mesh=mesh,
        in_specs=placed,
        out_specs=P("groups", None, "tensor"),
        check_vma=False,
    )
```

time: 384 us -> 175 us (0.46); the launches traced: 377 us -> 174 us
  waiting for transfers between devices: 241 us -> 57.1 us
  Pallas kernels: 0 us -> 55 us
  local copies, waits for them, and re-layouts: 54.2 us -> 15.6 us
  starting transfers between devices: 13.9 us -> 40.6 us
  other arithmetic: 30.2 us -> 4.81 us
  matrix products: 23.5 us -> 0 us
  between operations: 14 us -> 0.56 us
    all_gather x2 -> x0, waiting for transfers between devices: 169 us -> none  [the longest x1 125 us: on_device(): lax.all_gather(w_kv, 'tensor', axis=0, tiled=True)]
    all_to_all x2 -> x0, waiting for transfers between devices: 71.4 us -> none  [the longest x1 40.2 us: on_device(): lax.all_to_all(outgoing, 'tensor', split_axis=0, concat_axis=2, tiled=True)]
    ppermute x0 -> x40, waiting for transfers between devices: none -> 57.1 us  [move(): return lax.ppermute(value, ('groups', 'tensor'), pairs)]
    pallas_call x0 -> x9, Pallas kernels: none -> 55 us  [the longest x3 28.5 us: project(): pl.pallas_call(functools.partial(project_kernel, acc is not None, granule...]
    ppermute x0 -> x40, starting transfers between devices: none -> 40.6 us  [move(): return lax.ppermute(value, ('groups', 'tensor'), pairs)]
    dot_general x6 -> x0, matrix products: 23.5 us -> none  [the longest x1 18.3 us: on_device(): jnp.dot(normed, lax.all_gather(w_kv, 'tensor', axis=0, tiled=True), prefe...]
    reshape x6 -> x5, local copies, waits for them, and re-layouts: 24.3 us -> 0.97 us  [the longest x1 0.69 us: on_device(): return out.reshape(slots, STEPS, w_out.shape[1])]
    all_to_all x2 -> x0, other arithmetic: 22.1 us -> none  [on_device(): lax.all_to_all(spread, 'tensor', split_axis=0, concat_axis=1, tiled=True)]
  transfers between devices with their start and end apart: 4 -> 40, of which waited for: 4 -> 16; matrix products, arithmetic and copies ran while one was open for 2% -> 5% of each run, Pallas kernels for 0% -> 21%
where the time goes in v1:
time: 175 us; the launch traced here: 174 us
  waiting for transfers between devices  57.1 us (33%)
  Pallas kernels  55 us (31%)
  starting transfers between devices  40.6 us (23%)
  local copies, waits for them, and re-layouts  15.6 us (9%)
  other arithmetic  4.81 us (3%)
    ppermute x40, waiting for transfers between devices, move(): return lax.ppermute(value, ('groups', 'tensor'), pairs)  57.1 us
    ppermute x40, starting transfers between devices, move(): return lax.ppermute(value, ('groups', 'tensor'), pairs)  40.6 us
    pallas_call x3, Pallas kernels, project(): pl.pallas_call(functools.partial(project_kernel, acc is not None, granule...  28.5 us
    unnamed x58, local copies, waits for them, and re-layouts  11.8 us
    pallas_call x1, Pallas kernels, attend(): pl.pallas_call(functools.partial(attend_kernel, granules, blocks), grid_s...  11.4 us
    pallas_call x1, Pallas kernels, row_scale(): pl.pallas_call(functools.partial(scale_kernel, 512), grid=(rows // tile,)...  7.13 us
    pallas_call x1, Pallas kernels, combine(): pl.pallas_call(functools.partial(combine_kernel, halves, blocks, slots),...  4.15 us
  transfers between devices with their start and end apart: 40, of which 16 were waited for; matrix products, arithmetic and copies ran while one was open for 5% of the time, Pallas kernels for 21%

profile of v1, /device:TPU:0, one launch (start us, length us, event | category | flops | bytes accessed | tf_op | source)
XLA Modules:
  0.0 173.7 jit_solution(5320601460154793152)
XLA Ops:
  0.0 2.5 %split.1 = (bf16[512,512]{1,0:T(8,128)(2,1)}, bf16[512,512]{1,0:T(8,128)(2,1)}, bf16[256,512]{1,0:T(8,128)(2,1)}, bf16[256,512]{1,0:T(8,128)(2,1)}) custom-call(s32[1]{0:T(128)} %bitcast.66.core_ref.which_ref, s32[1]{0:T(128)} %bitcast.67.half_ref, bf16[512,1024]{1,0:T(8,128)(2,1)} %d.1, bf16[512,1024]{1,0:T(8,128)(2,1)} %d.1, bf16[512,1024]{1,0:T(8,128)(2,1)} %d.1, ...), custom_call_target="tpu_custom_call" | custom-call | tf_op jit(solution)/shard_map/split/pallas_call | solution.py:73
  2.6 2.4 %collective-permute-start = (bf16[256,512]{1,0:T(8,128)(2,1)}, bf16[256,512]{1,0:T(8,128)(2,1)S(1)}, u32[]{:S(2)}, u32[]{:S(2)}) collective-permute-start(bf16[256,512]{1,0:T(8,128)(2,1)} %get-tuple-element.24), channel_id=1, source_target_pairs={{0,3},{1,2},{2,1},{3,0},{4,7},{5,6},{6,5},{7,4},{8,11},{9,10},{10,... | collective-permute-start | bytes 786440 | tf_op jit(solution)/shard_map/yC/ppermute | solution.py:52
  6.8 5.2 %collective-permute-done.refs_43_ = bf16[256,512]{1,0:T(8,128)(2,1)S(1)} collective-permute-done((bf16[256,512]{1,0:T(8,128)(2,1)}, bf16[256,512]{1,0:T(8,128)(2,1)S(1)}, u32[]{:S(2)}, u32[]{:S(2)}) %collective-permute-start) | collective-permute-done | bytes 262176 | tf_op jit(solution)/shard_map/yC/ppermute | solution.py:52
  12.1 2.4 %collective-permute-start.4 = (bf16[256,512]{1,0:T(8,128)(2,1)}, bf16[256,512]{1,0:T(8,128)(2,1)S(1)}, u32[]{:S(2)}, u32[]{:S(2)}) collective-permute-start(bf16[256,512]{1,0:T(8,128)(2,1)} %get-tuple-element.27), channel_id=1, source_target_pairs={{0,4},{1,5},{2,6},{3,7},{4,8},{5,9},{6,10},{7,11},{8,12},{9,13},{1... | collective-permute-start | bytes 786440 | tf_op jit(solution)/shard_map/zB1/ppermute | solution.py:52
  14.6 1.6 collective-permute-start.8
  16.8 6.8 %collective-permute-done.4.refs_41_ = bf16[256,512]{1,0:T(8,128)(2,1)S(1)} collective-permute-done((bf16[256,512]{1,0:T(8,128)(2,1)}, bf16[256,512]{1,0:T(8,128)(2,1)S(1)}, u32[]{:S(2)}, u32[]{:S(2)}) %collective-permute-start.4) | collective-permute-done | bytes 262176 | tf_op jit(solution)/shard_map/zB1/ppermute | solution.py:52
  23.8 1.3 collective-permute-start.3
  25.2 9.1 %collective-permute-done.10.refs_29_ = bf16[256,512]{1,0:T(8,128)(2,1)S(1)} collective-permute-done((bf16[256,512]{1,0:T(8,128)(2,1)S(1)}, bf16[256,512]{1,0:T(8,128)(2,1)S(1)}, u32[]{:S(2)}, u32[]{:S(2)}) %collective-permute-start.10) | collective-permute-done | bytes 262176 | tf_op jit(solution)/shard_map/zB2/ppermute | solution.py:52
  34.3 1.2 collective-permute-start.9
  35.5 1.6 collective-permute-start.19
  37.6 2.4 %collective-permute-done.19 = bf16[2,2,80,128]{3,2,1,0:T(8,128)(2,1)S(1)} collective-permute-done((bf16[2,2,80,128]{3,2,1,0:T(8,128)(2,1)S(1)}, bf16[2,2,80,128]{3,2,1,0:T(8,128)(2,1)S(1)}, u32[]{:S(2)}, u32[]{:S(2)}) %collective-permute-start.19) | collective-permute-done | bytes 81952 | tf_op jit(solution)/shard_map/yq0/ppermute | solution.py:52
  40.0 2.0 %collective-permute-start.5 = (bf16[256,512]{1,0:T(8,128)(2,1)S(1)}, bf16[256,512]{1,0:T(8,128)(2,1)S(1)}, u32[]{:S(2)}, u32[]{:S(2)}) collective-permute-start(bf16[256,512]{1,0:T(8,128)(2,1)S(1)} %collective-permute-done.4.refs_41_), channel_id=1, source_target_pairs={{0,2},{1,3},{2,0},{3,1},{4,6},{5,7},{6,4},{7,5},{8,10},{9,11},{10,... | collective-permute-start | bytes 786440 | tf_op jit(solution)/shard_map/yBz1/ppermute | solution.py:52
  45.8 3.4 %collective-permute-done.5.refs_27_ = bf16[256,512]{1,0:T(8,128)(2,1)S(1)} collective-permute-done((bf16[256,512]{1,0:T(8,128)(2,1)S(1)}, bf16[256,512]{1,0:T(8,128)(2,1)S(1)}, u32[]{:S(2)}, u32[]{:S(2)}) %collective-permute-start.5) | collective-permute-done | bytes 262176 | tf_op jit(solution)/shard_map/yBz1/ppermute | solution.py:52
  50.6 2.0 %collective-permute-start.17 = (bf16[256,512]{1,0:T(8,128)(2,1)S(1)}, bf16[256,512]{1,0:T(8,128)(2,1)S(1)}, u32[]{:S(2)}, u32[]{:S(2)}) collective-permute-start(bf16[256,512]{1,0:T(8,128)(2,1)S(1)} %collective-permute-done.10.refs_29_), channel_id=1, source_target_pairs={{0,2},{1,3},{2,0},{3,1},{4,6},{5,7},{6,4},{7,5},{8,10},{9,11},{10,... | collective-permute-start | bytes 786440 | tf_op jit(solution)/shard_map/yBz2/ppermute | solution.py:52
  52.7 2.1 %collective-permute-done.14.refs_28_ = bf16[256,512]{1,0:T(8,128)(2,1)S(1)} collective-permute-done((bf16[256,512]{1,0:T(8,128)(2,1)S(1)}, bf16[256,512]{1,0:T(8,128)(2,1)S(1)}, u32[]{:S(2)}, u32[]{:S(2)}) %collective-permute-start.14) | collective-permute-done | bytes 262176 | tf_op jit(solution)/shard_map/yBx1/ppermute | solution.py:52
  56.4 4.5 %collective-permute-done.12.refs_45_ = bf16[512,512]{1,0:T(8,128)(2,1)S(1)} collective-permute-done((bf16[512,512]{1,0:T(8,128)(2,1)}, bf16[512,512]{1,0:T(8,128)(2,1)S(1)}, u32[]{:S(2)}, u32[]{:S(2)}) %collective-permute-start.12) | collective-permute-done | bytes 524320 | tf_op jit(solution)/shard_map/zC1/ppermute | solution.py:52
  61.6 1.3 collective-permute-start.16
  62.9 7.1 %row_scale.1.refs_36_.refs_25_.refs_13_ = f32[768,128]{1,0:T(8,128)S(1)} custom-call(bf16[768,8192]{1,0:T(8,128)(2,1)} %refs_4_.7), custom_call_target="tpu_custom_call" | custom-call | flops 12582912 | bytes 12582912 | tf_op jit(solution)/shard_map/stat/row_scale/pallas_call | solution.py:106
  71.3 1.2 gather_fusion
  73.4 1.6 maximum_bitcast_fusion
  74.9 1.6 maximum_bitcast_fusion.1
  76.5 2.7 %collective-permute-done.21.refs_30_ = bf16[256,512]{1,0:T(8,128)(2,1)} collective-permute-done((bf16[256,512]{1,0:T(8,128)(2,1)}, bf16[256,512]{1,0:T(8,128)(2,1)}, u32[]{:S(2)}, u32[]{:S(2)}) %collective-permute-start.21) | collective-permute-done | bytes 262176 | tf_op jit(solution)/shard_map/xB3/ppermute | solution.py:52
  79.2 1.4 collective-permute-start.18
  82.8 0.9 copy-done.12
  85.7 11.2 %project.3.refs_0_ = f32[1536,512]{1,0:T(8,128)} custom-call(s32[12]{0:T(128)S(1)} %stack.331.offs_ref, bf16[768,8192]{1,0:T(8,128)(2,1)} %refs_4_.7, bf16[768,8192]{1,0:T(8,128)(2,1)} %refs_4_.7, bf16[768,8192]{1,0:T(8,128)(2,1)} %refs_4_.7, bf16[768,8192]{1,0:T(8,128)(2,1)} %refs_4_.7, bf16[768,8192]{1,0:T(8,128)(2,1)} %refs_4_.7, ...), custom_call_target="tpu_custom_call" | custom-call | flops 4831838208 | bytes 3145728 | tf_op jit(solution)/shard_map/G1/project/pallas_call | solution.py:193
  96.9 1.4 collective-permute-done.25
  98.3 1.4 collective-permute-start.26
  99.6 8.8 %project.4.refs_0_ = f32[1536,512]{1,0:T(8,128)S(1)} custom-call(s32[8]{0:T(128)S(1)} %stack.318.offs_ref, f32[1536,512]{1,0:T(8,128)} %project.3.refs_0_, bf16[768,8192]{1,0:T(8,128)(2,1)} %refs_4_.7, bf16[768,8192]{1,0:T(8,128)(2,1)} %refs_4_.7, bf16[768,8192]{1,0:T(8,128)(2,1)} %refs_4_.7, bf16[768,8192]{1,0:T(8,128)(2,1)} %refs_4_.7, ...), custom_call_target="tpu_custom_call" | custom-call | flops 3221225472 | bytes 3145728 | tf_op jit(solution)/shard_map/G2/project/pallas_call | solution.py:193
  108.4 1.6 copy-done.3
  110.1 2.4 %collective-permute-start.30 = (bf16[2,2,80,128]{3,2,1,0:T(8,128)(2,1)S(1)}, bf16[2,2,80,128]{3,2,1,0:T(8,128)(2,1)S(1)}, u32[]{:S(2)}, u32[]{:S(2)}) collective-permute-start(bf16[2,2,80,128]{3,2,1,0:T(8,128)(2,1)S(1)} %collective-permute-done.25), channel_id=1, source_target_pairs={{0,4},{1,5},{2,6},{3,7},{4,8},{5,9},{6,10},{7,11},{8,12},{9,13},{1... | collective-permute-start | bytes 245768 | tf_op jit(solution)/shard_map/zq3/ppermute | solution.py:52
  112.5 1.1 collective-permute-start.29
  113.6 1.3 collective-permute-start.28
  114.9 8.5 %project.5.refs_0_ = f32[1536,512]{1,0:T(8,128)S(1)} custom-call(s32[8]{0:T(128)S(1)} %stack.309.offs_ref, f32[1536,512]{1,0:T(8,128)} %copy-done.3, bf16[768,8192]{1,0:T(8,128)(2,1)} %refs_4_.7, bf16[768,8192]{1,0:T(8,128)(2,1)} %refs_4_.7, bf16[768,8192]{1,0:T(8,128)(2,1)} %refs_4_.7, bf16[768,8192]{1,0:T(8,128)(2,1)} %refs_4_.7, ...), custom_call_target="tpu_custom_call" | custom-call | flops 3221225472 | bytes 3145728 | tf_op jit(solution)/shard_map/G3/project/pallas_call | solution.py:193
  123.5 1.4 collective-permute-start.31
  124.9 3.0 %collective-permute-done.31 = bf16[2,2,80,128]{3,2,1,0:T(8,128)(2,1)S(1)} collective-permute-done((bf16[2,2,80,128]{3,2,1,0:T(8,128)(2,1)S(1)}, bf16[2,2,80,128]{3,2,1,0:T(8,128)(2,1)S(1)}, u32[]{:S(2)}, u32[]{:S(2)}) %collective-permute-start.31) | collective-permute-done | bytes 81952 | tf_op jit(solution)/shard_map/yq3/ppermute | solution.py:52
  128.1 11.4 %attend.1.refs_0_ = bf16[2,400,128]{2,1,0:T(8,128)(2,1)S(1)} custom-call(s32[4]{0:T(128)S(1)} %pad_add_fusion.3.offs_ref, s32[12,3]{1,0:T(8,128)S(1)} %copy.19.table_ref, f32[1536,512]{1,0:T(8,128)S(1)} %project.5.refs_0_, bf16[768,8192]{1,0:T(8,128)(2,1)} %refs_4_.7, bf16[768,8192]{1,0:T(8,128)(2,1)} %refs_4_.7, bf16[768,8192]{1,0:T(8,128)(2,1)} %refs_4_.7, ...), custom_call_target="tpu_custom_call" | custom-call | flops 1610612736 | bytes 3145728 | tf_op jit(solution)/shard_map/attend/pallas_call | solution.py:302
  139.6 0.9 collective-permute-start.33
  140.6 2.8 %collective-permute-start.34 = (bf16[2,400,128]{2,1,0:T(8,128)(2,1)S(1)}, bf16[2,400,128]{2,1,0:T(8,128)(2,1)S(1)}, u32[]{:S(2)}, u32[]{:S(2)}) collective-permute-start(bf16[2,400,128]{2,1,0:T(8,128)(2,1)S(1)} %attend.1.refs_0_), channel_id=1, source_target_pairs={{0,12},{1,13},{2,14},{3,15},{4,0},{5,1},{6,2},{7,3},{8,4},{9,5},{1... | collective-permute-start | bytes 614408 | tf_op jit(solution)/shard_map/oz3/ppermute | solution.py:52
  143.4 1.4 collective-permute-start.35
  144.8 4.4 %collective-permute-done.32.refs_1_ = bf16[2,400,128]{2,1,0:T(8,128)(2,1)S(1)} collective-permute-done((bf16[2,400,128]{2,1,0:T(8,128)(2,1)S(1)}, bf16[2,400,128]{2,1,0:T(8,128)(2,1)S(1)}, u32[]{:S(2)}, u32[]{:S(2)}) %collective-permute-start.32) | collective-permute-done | bytes 204832 | tf_op jit(solution)/shard_map/oz1/ppermute | solution.py:52
  149.2 1.4 collective-permute-start.36
  150.6 3.1 %collective-permute-done.33.refs_2_ = bf16[2,400,128]{2,1,0:T(8,128)(2,1)S(1)} collective-permute-done((bf16[2,400,128]{2,1,0:T(8,128)(2,1)S(1)}, bf16[2,400,128]{2,1,0:T(8,128)(2,1)S(1)}, u32[]{:S(2)}, u32[]{:S(2)}) %collective-permute-start.33) | collective-permute-done | bytes 204832 | tf_op jit(solution)/shard_map/oz2/ppermute | solution.py:52
  153.7 1.4 collective-permute-start.37
  156.0 5.5 %collective-permute-done.37.refs_6_ = bf16[2,400,128]{2,1,0:T(8,128)(2,1)S(1)} collective-permute-done((bf16[2,400,128]{2,1,0:T(8,128)(2,1)S(1)}, bf16[2,400,128]{2,1,0:T(8,128)(2,1)S(1)}, u32[]{:S(2)}, u32[]{:S(2)}) %collective-permute-start.37) | collective-permute-done | bytes 204832 | tf_op jit(solution)/shard_map/oy2/ppermute | solution.py:52
  161.5 2.2 %collective-permute-done.38.refs_7_ = bf16[2,400,128]{2,1,0:T(8,128)(2,1)S(1)} collective-permute-done((bf16[2,400,128]{2,1,0:T(8,128)(2,1)S(1)}, bf16[2,400,128]{2,1,0:T(8,128)(2,1)S(1)}, u32[]{:S(2)}, u32[]{:S(2)}) %collective-permute-start.38) | collective-permute-done | bytes 204832 | tf_op jit(solution)/shard_map/oy3/ppermute | solution.py:52
  163.7 4.1 %combine.1.x_ref = bf16[16,128,128]{2,1,0:T(8,128)(2,1)S(1)} custom-call(s32[128]{0:T(128)S(1)} %reshape.790.slot_ref, s32[1,128]{1,0:T(1,128)S(1)} %reshape_reshape.3.slot_row_ref, bf16[2,400,128]{2,1,0:T(8,128)(2,1)S(1)} %attend.1.refs_0_, bf16[2,400,128]{2,1,0:T(8,128)(2,1)S(1)} %collective-permute-done.32.refs_1_, ...), custom_call_target="tpu_custom_call" | custom-call | tf_op jit(solution)/shard_map/combine/pallas_call | solution.py:364
  168.0 2.2 %copy-done.1 = bf16[4096,512]{1,0:T(8,128)(2,1)S(1)} copy-done((bf16[4096,512]{1,0:T(8,128)(2,1)S(1)}, bf16[4096,512]{1,0:T(8,128)(2,1)}, u32[]{:S(2)}) %copy-start.1) | copy-done | bytes 4194328
  170.9 1.5 copy-done.2
  (146 shorter events, 20.4 us)
Async XLA Ops:
  0.0 16.5 %copy-start.25 = (s32[96]{0:T(128)S(1)}, s32[96]{0:T(128)}, u32[]{:S(2)}) copy-start(s32[96]{0:T(128)} %param.15) | copy-start | bytes 1156
  2.6 9.4 %collective-permute-start = (bf16[256,512]{1,0:T(8,128)(2,1)}, bf16[256,512]{1,0:T(8,128)(2,1)S(1)}, u32[]{:S(2)}, u32[]{:S(2)}) collective-permute-start(bf16[256,512]{1,0:T(8,128)(2,1)} %get-tuple-element.24), channel_id=1, source_target_pairs={{0,3},{1,2},{2,1},{3,0},{4,7},{5,6},{6,5},{7,4},{8,11},{9,10},{10,... | collective-permute-start | bytes 786440 | tf_op jit(solution)/shard_map/yC/ppermute | solution.py:52
  5.2 1.6 collective-permute-start.1
  12.0 70.1 %collective-permute-start.2 = (bf16[768,8192]{1,0:T(8,128)(2,1)}, bf16[768,8192]{1,0:T(8,128)(2,1)}, u32[]{:S(2)}, u32[]{:S(2)}) collective-permute-start(bf16[768,8192]{1,0:T(8,128)(2,1)} %refs_4_.7), channel_id=1, source_target_pairs={{0,1},{1,0},{2,3},{3,2},{4,5},{5,4},{6,7},{7,6},{8,9},{9,8},{10,11... | collective-permute-start | bytes 37748744 | tf_op jit(solution)/shard_map/ex/ppermute | solution.py:52
  12.1 11.5 %collective-permute-start.4 = (bf16[256,512]{1,0:T(8,128)(2,1)}, bf16[256,512]{1,0:T(8,128)(2,1)S(1)}, u32[]{:S(2)}, u32[]{:S(2)}) collective-permute-start(bf16[256,512]{1,0:T(8,128)(2,1)} %get-tuple-element.27), channel_id=1, source_target_pairs={{0,4},{1,5},{2,6},{3,7},{4,8},{5,9},{6,10},{7,11},{8,12},{9,13},{1... | collective-permute-start | bytes 786440 | tf_op jit(solution)/shard_map/zB1/ppermute | solution.py:52
  14.5 22.6 %collective-permute-start.7 = (bf16[512,512]{1,0:T(8,128)(2,1)}, bf16[512,512]{1,0:T(8,128)(2,1)S(1)}, u32[]{:S(2)}, u32[]{:S(2)}) collective-permute-start(bf16[512,512]{1,0:T(8,128)(2,1)} %get-tuple-element.30), channel_id=1, source_target_pairs={{0,1},{1,0},{2,3},{3,2},{4,5},{5,4},{6,7},{7,6},{8,9},{9,8},{10,11... | collective-permute-start | bytes 1572872 | tf_op jit(solution)/shard_map/c/ppermute | solution.py:52
  14.6 29.4 %collective-permute-start.8 = (bf16[512,512]{1,0:T(8,128)(2,1)}, bf16[512,512]{1,0:T(8,128)(2,1)S(1)}, u32[]{:S(2)}, u32[]{:S(2)}) collective-permute-start(bf16[512,512]{1,0:T(8,128)(2,1)} %get-tuple-element.29.refs_38_), channel_id=1, source_target_pairs={{0,2},{1,3},{2,0},{3,1},{4,6},{5,7},{6,4},{7,5},{8,10},{9,11},{10,... | collective-permute-start | bytes 1572872 | tf_op jit(solution)/shard_map/yB0/ppermute | solution.py:52
  23.6 39.3 %copy-start.11 = (bf16[256,512]{1,0:T(8,128)(2,1)}, bf16[256,512]{1,0:T(8,128)(2,1)S(1)}, u32[]{:S(2)}) copy-start(bf16[256,512]{1,0:T(8,128)(2,1)S(1)} %collective-permute-done.4.refs_41_) | copy-start | bytes 786436
  23.6 10.7 %collective-permute-start.10 = (bf16[256,512]{1,0:T(8,128)(2,1)S(1)}, bf16[256,512]{1,0:T(8,128)(2,1)S(1)}, u32[]{:S(2)}, u32[]{:S(2)}) collective-permute-start(bf16[256,512]{1,0:T(8,128)(2,1)S(1)} %collective-permute-done.4.refs_41_), channel_id=1, source_target_pairs={{0,4},{1,5},{2,6},{3,7},{4,8},{5,9},{6,10},{7,11},{8,12},{9,13},{1... | collective-permute-start | bytes 786440 | tf_op jit(solution)/shard_map/zB2/ppermute | solution.py:52
  23.8 11.7 %collective-permute-start.3 = (bf16[2,2,80,128]{3,2,1,0:T(8,128)(2,1)S(1)}, bf16[2,2,80,128]{3,2,1,0:T(8,128)(2,1)S(1)}, u32[]{:S(2)}, u32[]{:S(2)}) collective-permute-start(bf16[2,2,80,128]{3,2,1,0:T(8,128)(2,1)S(1)} %get-tuple-element.44), channel_id=1, source_target_pairs={{0,4},{1,5},{2,6},{3,7},{4,8},{5,9},{6,10},{7,11},{8,12},{9,13},{1... | collective-permute-start | bytes 245768 | tf_op jit(solution)/shard_map/zq1/ppermute | solution.py:52
  34.3 9.8 %collective-permute-start.9 = (bf16[256,512]{1,0:T(8,128)(2,1)S(1)}, bf16[256,512]{1,0:T(8,128)(2,1)S(1)}, u32[]{:S(2)}, u32[]{:S(2)}) collective-permute-start(bf16[256,512]{1,0:T(8,128)(2,1)S(1)} %collective-permute-done.4.refs_41_), channel_id=1, source_target_pairs={{0,16},{1,17},{2,18},{3,19},{4,20},{5,21},{6,22},{7,23},{8,24},{9,... | collective-permute-start | bytes 786440 | tf_op jit(solution)/shard_map/xB1/ppermute | solution.py:52
  35.5 4.5 %collective-permute-start.19 = (bf16[2,2,80,128]{3,2,1,0:T(8,128)(2,1)S(1)}, bf16[2,2,80,128]{3,2,1,0:T(8,128)(2,1)S(1)}, u32[]{:S(2)}, u32[]{:S(2)}) collective-permute-start(bf16[2,2,80,128]{3,2,1,0:T(8,128)(2,1)S(1)} %get-tuple-element.44), channel_id=1, source_target_pairs={{0,2},{1,3},{2,0},{3,1},{4,6},{5,7},{6,4},{7,5},{8,10},{9,11},{10,... | collective-permute-start | bytes 245768 | tf_op jit(solution)/shard_map/yq0/ppermute | solution.py:52
  37.1 5.3 %collective-permute-start.22 = (bf16[2,2,80,128]{3,2,1,0:T(8,128)(2,1)S(1)}, bf16[2,2,80,128]{3,2,1,0:T(8,128)(2,1)S(1)}, u32[]{:S(2)}, u32[]{:S(2)}) collective-permute-start(bf16[2,2,80,128]{3,2,1,0:T(8,128)(2,1)S(1)} %collective-permute-done.3), channel_id=1, source_target_pairs={{0,2},{1,3},{2,0},{3,1},{4,6},{5,7},{6,4},{7,5},{8,10},{9,11},{10,... | collective-permute-start | bytes 245768 | tf_op jit(solution)/shard_map/yq1/ppermute | solution.py:52
  40.0 9.2 %collective-permute-start.5 = (bf16[256,512]{1,0:T(8,128)(2,1)S(1)}, bf16[256,512]{1,0:T(8,128)(2,1)S(1)}, u32[]{:S(2)}, u32[]{:S(2)}) collective-permute-start(bf16[256,512]{1,0:T(8,128)(2,1)S(1)} %collective-permute-done.4.refs_41_), channel_id=1, source_target_pairs={{0,2},{1,3},{2,0},{3,1},{4,6},{5,7},{6,4},{7,5},{8,10},{9,11},{10,... | collective-permute-start | bytes 786440 | tf_op jit(solution)/shard_map/yBz1/ppermute | solution.py:52
  42.4 7.6 %collective-permute-start.11 = (bf16[256,512]{1,0:T(8,128)(2,1)S(1)}, bf16[256,512]{1,0:T(8,128)(2,1)S(1)}, u32[]{:S(2)}, u32[]{:S(2)}) collective-permute-start(bf16[256,512]{1,0:T(8,128)(2,1)S(1)} %collective-permute-done.refs_43_), channel_id=1, source_target_pairs={{0,16},{1,17},{2,18},{3,19},{4,20},{5,21},{6,22},{7,23},{8,24},{9,... | collective-permute-start | bytes 786440 | tf_op jit(solution)/shard_map/xC0/ppermute | solution.py:52
  44.0 16.9 %collective-permute-start.12 = (bf16[512,512]{1,0:T(8,128)(2,1)}, bf16[512,512]{1,0:T(8,128)(2,1)S(1)}, u32[]{:S(2)}, u32[]{:S(2)}) collective-permute-start(bf16[512,512]{1,0:T(8,128)(2,1)} %pad_maximum_fusion.1), channel_id=1, source_target_pairs={{0,4},{1,5},{2,6},{3,7},{4,8},{5,9},{6,10},{7,11},{8,12},{9,13},{1... | collective-permute-start | bytes 1572872 | tf_op jit(solution)/shard_map/zC1/ppermute | solution.py:52
  44.1 10.8 %collective-permute-start.14 = (bf16[256,512]{1,0:T(8,128)(2,1)S(1)}, bf16[256,512]{1,0:T(8,128)(2,1)S(1)}, u32[]{:S(2)}, u32[]{:S(2)}) collective-permute-start(bf16[256,512]{1,0:T(8,128)(2,1)S(1)} %collective-permute-done.9.refs_42_), channel_id=1, source_target_pairs={{0,2},{1,3},{2,0},{3,1},{4,6},{5,7},{6,4},{7,5},{8,10},{9,11},{10,... | collective-permute-start | bytes 786440 | tf_op jit(solution)/shard_map/yBx1/ppermute | solution.py:52
  49.9 20.1 %collective-permute-start.20 = (bf16[256,512]{1,0:T(8,128)(2,1)S(1)}, bf16[256,512]{1,0:T(8,128)(2,1)}, u32[]{:S(2)}, u32[]{:S(2)}) collective-permute-start(bf16[256,512]{1,0:T(8,128)(2,1)S(1)} %collective-permute-done.10.refs_29_), channel_id=1, source_target_pairs={{0,4},{1,5},{2,6},{3,7},{4,8},{5,9},{6,10},{7,11},{8,12},{9,13},{1... | collective-permute-start | bytes 786440 | tf_op jit(solution)/shard_map/zB3/ppermute | solution.py:52
  50.6 10.3 %collective-permute-start.17 = (bf16[256,512]{1,0:T(8,128)(2,1)S(1)}, bf16[256,512]{1,0:T(8,128)(2,1)S(1)}, u32[]{:S(2)}, u32[]{:S(2)}) collective-permute-start(bf16[256,512]{1,0:T(8,128)(2,1)S(1)} %collective-permute-done.10.refs_29_), channel_id=1, source_target_pairs={{0,2},{1,3},{2,0},{3,1},{4,6},{5,7},{6,4},{7,5},{8,10},{9,11},{10,... | collective-permute-start | bytes 786440 | tf_op jit(solution)/shard_map/yBz2/ppermute | solution.py:52
  55.5 14.6 %collective-permute-start.13 = (bf16[256,512]{1,0:T(8,128)(2,1)S(1)}, bf16[256,512]{1,0:T(8,128)(2,1)}, u32[]{:S(2)}, u32[]{:S(2)}) collective-permute-start(bf16[256,512]{1,0:T(8,128)(2,1)S(1)} %collective-permute-done.10.refs_29_), channel_id=1, source_target_pairs={{0,16},{1,17},{2,18},{3,19},{4,20},{5,21},{6,22},{7,23},{8,24},{9,... | collective-permute-start | bytes 786440 | tf_op jit(solution)/shard_map/xB2/ppermute | solution.py:52
  60.9 19.7 %collective-permute-start.15 = (bf16[512,512]{1,0:T(8,128)(2,1)S(1)}, bf16[512,512]{1,0:T(8,128)(2,1)}, u32[]{:S(2)}, u32[]{:S(2)}) collective-permute-start(bf16[512,512]{1,0:T(8,128)(2,1)S(1)} %collective-permute-done.12.refs_45_), channel_id=1, source_target_pairs={{0,4},{1,5},{2,6},{3,7},{4,8},{5,9},{6,10},{7,11},{8,12},{9,13},{1... | collective-permute-start | bytes 1572872 | tf_op jit(solution)/shard_map/zC2/ppermute | solution.py:52
  61.6 19.7 %collective-permute-start.16 = (bf16[512,512]{1,0:T(8,128)(2,1)S(1)}, bf16[512,512]{1,0:T(8,128)(2,1)}, u32[]{:S(2)}, u32[]{:S(2)}) collective-permute-start(bf16[512,512]{1,0:T(8,128)(2,1)S(1)} %collective-permute-done.12.refs_45_), channel_id=1, source_target_pairs={{0,16},{1,17},{2,18},{3,19},{4,20},{5,21},{6,22},{7,23},{8,24},{9,... | collective-permute-start | bytes 1572872 | tf_op jit(solution)/shard_map/xC1/ppermute | solution.py:52
  62.9 19.9 %copy-start = (f32[8192]{0:T(1024)S(1)}, f32[8192]{0:T(1024)}, u32[]{:S(2)}) copy-start(f32[8192]{0:T(1024)} %param.10) | copy-start | bytes 98308
  62.9 19.9 %copy-start.4 = (bf16[512,512]{1,0:T(8,128)(2,1)S(1)}, bf16[512,512]{1,0:T(8,128)(2,1)}, u32[]{:S(2)}) copy-start(bf16[512,512]{1,0:T(8,128)(2,1)} %get-tuple-element.29.refs_38_) | copy-start | bytes 1572868
  70.1 11.2 %collective-permute-start.6 = (f32[768,128]{1,0:T(8,128)S(1)}, f32[768,128]{1,0:T(8,128)S(1)}, u32[]{:S(2)}, u32[]{:S(2)}) collective-permute-start(f32[768,128]{1,0:T(8,128)S(1)} %row_scale.1.refs_36_.refs_25_.refs_13_), channel_id=1, source_target_pairs={{0,1},{1,0},{2,3},{3,2},{4,5},{5,4},{6,7},{7,6},{8,9},{9,8},{10,11... | collective-permute-start | bytes 1179656 | tf_op jit(solution)/shard_map/inv/ppermute | solution.py:52
  70.2 9.1 %collective-permute-start.21 = (bf16[256,512]{1,0:T(8,128)(2,1)}, bf16[256,512]{1,0:T(8,128)(2,1)}, u32[]{:S(2)}, u32[]{:S(2)}) collective-permute-start(bf16[256,512]{1,0:T(8,128)(2,1)} %collective-permute-done.20.refs_29_), channel_id=1, source_target_pairs={{0,16},{1,17},{2,18},{3,19},{4,20},{5,21},{6,22},{7,23},{8,24},{9,... | collective-permute-start | bytes 786440 | tf_op jit(solution)/shard_map/xB3/ppermute | solution.py:52
  79.2 35.7 %collective-permute-start.18 = (bf16[256,512]{1,0:T(8,128)(2,1)}, bf16[256,512]{1,0:T(8,128)(2,1)S(1)}, u32[]{:S(2)}, u32[]{:S(2)}) collective-permute-start(bf16[256,512]{1,0:T(8,128)(2,1)} %collective-permute-done.13.refs_30_), channel_id=1, source_target_pairs={{0,2},{1,3},{2,0},{3,1},{4,6},{5,7},{6,4},{7,5},{8,10},{9,11},{10,... | collective-permute-start | bytes 786440 | tf_op jit(solution)/shard_map/yBx2/ppermute | solution.py:52
  80.6 47.5 %collective-permute-start.27 = (bf16[256,512]{1,0:T(8,128)(2,1)}, bf16[256,512]{1,0:T(8,128)(2,1)}, u32[]{:S(2)}, u32[]{:S(2)}) collective-permute-start(bf16[256,512]{1,0:T(8,128)(2,1)} %collective-permute-done.21.refs_30_), channel_id=1, source_target_pairs={{0,2},{1,3},{2,0},{3,1},{4,6},{5,7},{6,4},{7,5},{8,10},{9,11},{10,... | collective-permute-start | bytes 786440 | tf_op jit(solution)/shard_map/yBx3/ppermute | solution.py:52
  81.3 31.2 %collective-permute-start.23 = (bf16[512,512]{1,0:T(8,128)(2,1)}, bf16[512,512]{1,0:T(8,128)(2,1)S(1)}, u32[]{:S(2)}, u32[]{:S(2)}) collective-permute-start(bf16[512,512]{1,0:T(8,128)(2,1)} %collective-permute-done.15.refs_31_), channel_id=1, source_target_pairs={{0,4},{1,5},{2,6},{3,7},{4,8},{5,9},{6,10},{7,11},{8,12},{9,13},{1... | collective-permute-start | bytes 1572872 | tf_op jit(solution)/shard_map/zC3/ppermute | solution.py:52
  81.3 28.8 %collective-permute-start.24 = (bf16[512,512]{1,0:T(8,128)(2,1)}, bf16[512,512]{1,0:T(8,128)(2,1)S(1)}, u32[]{:S(2)}, u32[]{:S(2)}) collective-permute-start(bf16[512,512]{1,0:T(8,128)(2,1)} %collective-permute-done.15.refs_31_), channel_id=1, source_target_pairs={{0,16},{1,17},{2,18},{3,19},{4,20},{5,21},{6,22},{7,23},{8,24},{9,... | collective-permute-start | bytes 1572872 | tf_op jit(solution)/shard_map/xC2/ppermute | solution.py:52
  82.1 16.1 %collective-permute-start.25 = (bf16[2,2,80,128]{3,2,1,0:T(8,128)(2,1)}, bf16[2,2,80,128]{3,2,1,0:T(8,128)(2,1)S(1)}, u32[]{:S(2)}, u32[]{:S(2)}) collective-permute-start(bf16[2,2,80,128]{3,2,1,0:T(8,128)(2,1)} %copy-done.19), channel_id=1, source_target_pairs={{0,4},{1,5},{2,6},{3,7},{4,8},{5,9},{6,10},{7,11},{8,12},{9,13},{1... | collective-permute-start | bytes 245768 | tf_op jit(solution)/shard_map/zq2/ppermute | solution.py:52
  96.9 18.0 %copy-start.10 = (bf16[256,512]{1,0:T(8,128)(2,1)S(1)}, bf16[256,512]{1,0:T(8,128)(2,1)}, u32[]{:S(2)}) copy-start(bf16[256,512]{1,0:T(8,128)(2,1)} %copy-done.9) | copy-start | bytes 786436
  98.3 15.4 %collective-permute-start.26 = (bf16[256,512]{1,0:T(8,128)(2,1)}, bf16[256,512]{1,0:T(8,128)(2,1)S(1)}, u32[]{:S(2)}, u32[]{:S(2)}) collective-permute-start(bf16[256,512]{1,0:T(8,128)(2,1)} %collective-permute-done.20.refs_29_), channel_id=1, source_target_pairs={{0,2},{1,3},{2,0},{3,1},{4,6},{5,7},{6,4},{7,5},{8,10},{9,11},{10,... | collective-permute-start | bytes 786440 | tf_op jit(solution)/shard_map/yBz3/ppermute | solution.py:52
  110.1 17.9 %copy-start.17 = (bf16[1,2,2,2,80,128]{5,4,3,2,1,0:T(8,128)(2,1)S(1)}, bf16[1,2,2,2,80,128]{5,4,3,2,1,0:T(8,128)(2,1)}, u32[]{:S(2)}) copy-start(bf16[1,2,2,2,80,128]{5,4,3,2,1,0:T(8,128)(2,1)} %maximum_bitcast_fusion) | copy-start | bytes 491524
  110.1 17.9 %copy-start.18 = (bf16[1,2,2,2,80,128]{5,4,3,2,1,0:T(8,128)(2,1)S(1)}, bf16[1,2,2,2,80,128]{5,4,3,2,1,0:T(8,128)(2,1)}, u32[]{:S(2)}) copy-start(bf16[1,2,2,2,80,128]{5,4,3,2,1,0:T(8,128)(2,1)} %maximum_bitcast_fusion.1) | copy-start | bytes 491524
  110.1 13.4 %collective-permute-start.30 = (bf16[2,2,80,128]{3,2,1,0:T(8,128)(2,1)S(1)}, bf16[2,2,80,128]{3,2,1,0:T(8,128)(2,1)S(1)}, u32[]{:S(2)}, u32[]{:S(2)}) collective-permute-start(bf16[2,2,80,128]{3,2,1,0:T(8,128)(2,1)S(1)} %collective-permute-done.25), channel_id=1, source_target_pairs={{0,4},{1,5},{2,6},{3,7},{4,8},{5,9},{6,10},{7,11},{8,12},{9,13},{1... | collective-permute-start | bytes 245768 | tf_op jit(solution)/shard_map/zq3/ppermute | solution.py:52
  112.5 12.4 %collective-permute-start.29 = (bf16[2,2,80,128]{3,2,1,0:T(8,128)(2,1)S(1)}, bf16[2,2,80,128]{3,2,1,0:T(8,128)(2,1)S(1)}, u32[]{:S(2)}, u32[]{:S(2)}) collective-permute-start(bf16[2,2,80,128]{3,2,1,0:T(8,128)(2,1)S(1)} %collective-permute-done.25), channel_id=1, source_target_pairs={{0,2},{1,3},{2,0},{3,1},{4,6},{5,7},{6,4},{7,5},{8,10},{9,11},{10,... | collective-permute-start | bytes 245768 | tf_op jit(solution)/shard_map/yq2/ppermute | solution.py:52
  113.6 14.5 %collective-permute-start.28 = (bf16[512,512]{1,0:T(8,128)(2,1)S(1)}, bf16[512,512]{1,0:T(8,128)(2,1)S(1)}, u32[]{:S(2)}, u32[]{:S(2)}) collective-permute-start(bf16[512,512]{1,0:T(8,128)(2,1)S(1)} %collective-permute-done.23.refs_31_), channel_id=1, source_target_pairs={{0,16},{1,17},{2,18},{3,19},{4,20},{5,21},{6,22},{7,23},{8,24},{9,... | collective-permute-start | bytes 1572872 | tf_op jit(solution)/shard_map/xC3/ppermute | solution.py:52
  123.5 4.5 %collective-permute-start.31 = (bf16[2,2,80,128]{3,2,1,0:T(8,128)(2,1)S(1)}, bf16[2,2,80,128]{3,2,1,0:T(8,128)(2,1)S(1)}, u32[]{:S(2)}, u32[]{:S(2)}) collective-permute-start(bf16[2,2,80,128]{3,2,1,0:T(8,128)(2,1)S(1)} %collective-permute-done.30), channel_id=1, source_target_pairs={{0,2},{1,3},{2,0},{3,1},{4,6},{5,7},{6,4},{7,5},{8,10},{9,11},{10,... | collective-permute-start | bytes 245768 | tf_op jit(solution)/shard_map/yq3/ppermute | solution.py:52
  128.1 27.6 %copy-start.23 = (s32[16,6]{1,0:T(8,128)S(1)}, s32[16,6]{1,0:T(8,128)}, u32[]{:S(2)}) copy-start(s32[16,6]{1,0:T(8,128)} %gather_fusion) | copy-start | bytes 1156
  139.5 9.7 %collective-permute-start.32 = (bf16[2,400,128]{2,1,0:T(8,128)(2,1)S(1)}, bf16[2,400,128]{2,1,0:T(8,128)(2,1)S(1)}, u32[]{:S(2)}, u32[]{:S(2)}) collective-permute-start(bf16[2,400,128]{2,1,0:T(8,128)(2,1)S(1)} %attend.1.refs_0_), channel_id=1, source_target_pairs={{0,4},{1,5},{2,6},{3,7},{4,8},{5,9},{6,10},{7,11},{8,12},{9,13},{1... | collective-permute-start | bytes 614408 | tf_op jit(solution)/shard_map/oz1/ppermute | solution.py:52
  139.6 14.1 %collective-permute-start.33 = (bf16[2,400,128]{2,1,0:T(8,128)(2,1)S(1)}, bf16[2,400,128]{2,1,0:T(8,128)(2,1)S(1)}, u32[]{:S(2)}, u32[]{:S(2)}) collective-permute-start(bf16[2,400,128]{2,1,0:T(8,128)(2,1)S(1)} %attend.1.refs_0_), channel_id=1, source_target_pairs={{0,8},{1,9},{2,10},{3,11},{4,12},{5,13},{6,14},{7,15},{8,0},{9,1},... | collective-permute-start | bytes 614408 | tf_op jit(solution)/shard_map/oz2/ppermute | solution.py:52
  140.6 14.5 %collective-permute-start.34 = (bf16[2,400,128]{2,1,0:T(8,128)(2,1)S(1)}, bf16[2,400,128]{2,1,0:T(8,128)(2,1)S(1)}, u32[]{:S(2)}, u32[]{:S(2)}) collective-permute-start(bf16[2,400,128]{2,1,0:T(8,128)(2,1)S(1)} %attend.1.refs_0_), channel_id=1, source_target_pairs={{0,12},{1,13},{2,14},{3,15},{4,0},{5,1},{6,2},{7,3},{8,4},{9,5},{1... | collective-permute-start | bytes 614408 | tf_op jit(solution)/shard_map/oz3/ppermute | solution.py:52
  143.4 12.6 %collective-permute-start.35 = (bf16[2,400,128]{2,1,0:T(8,128)(2,1)S(1)}, bf16[2,400,128]{2,1,0:T(8,128)(2,1)S(1)}, u32[]{:S(2)}, u32[]{:S(2)}) collective-permute-start(bf16[2,400,128]{2,1,0:T(8,128)(2,1)S(1)} %attend.1.refs_0_), channel_id=1, source_target_pairs={{0,2},{1,3},{2,0},{3,1},{4,6},{5,7},{6,4},{7,5},{8,10},{9,11},{10,... | collective-permute-start | bytes 614408 | tf_op jit(solution)/shard_map/oy0/ppermute | solution.py:52
  149.2 6.8 %collective-permute-start.36 = (bf16[2,400,128]{2,1,0:T(8,128)(2,1)S(1)}, bf16[2,400,128]{2,1,0:T(8,128)(2,1)S(1)}, u32[]{:S(2)}, u32[]{:S(2)}) collective-permute-start(bf16[2,400,128]{2,1,0:T(8,128)(2,1)S(1)} %collective-permute-done.32.refs_1_), channel_id=1, source_target_pairs={{0,2},{1,3},{2,0},{3,1},{4,6},{5,7},{6,4},{7,5},{8,10},{9,11},{10,... | collective-permute-start | bytes 614408 | tf_op jit(solution)/shard_map/oy1/ppermute | solution.py:52
  153.7 7.9 %collective-permute-start.37 = (bf16[2,400,128]{2,1,0:T(8,128)(2,1)S(1)}, bf16[2,400,128]{2,1,0:T(8,128)(2,1)S(1)}, u32[]{:S(2)}, u32[]{:S(2)}) collective-permute-start(bf16[2,400,128]{2,1,0:T(8,128)(2,1)S(1)} %collective-permute-done.33.refs_2_), channel_id=1, source_target_pairs={{0,2},{1,3},{2,0},{3,1},{4,6},{5,7},{6,4},{7,5},{8,10},{9,11},{10,... | collective-permute-start | bytes 614408 | tf_op jit(solution)/shard_map/oy2/ppermute | solution.py:52
  155.1 8.7 %collective-permute-start.38 = (bf16[2,400,128]{2,1,0:T(8,128)(2,1)S(1)}, bf16[2,400,128]{2,1,0:T(8,128)(2,1)S(1)}, u32[]{:S(2)}, u32[]{:S(2)}) collective-permute-start(bf16[2,400,128]{2,1,0:T(8,128)(2,1)S(1)} %collective-permute-done.34.refs_3_), channel_id=1, source_target_pairs={{0,2},{1,3},{2,0},{3,1},{4,6},{5,7},{6,4},{7,5},{8,10},{9,11},{10,... | collective-permute-start | bytes 614408 | tf_op jit(solution)/shard_map/oy3/ppermute | solution.py:52
  167.9 3.0 %collective-permute-start.39 = (bf16[16,128,128]{2,1,0:T(8,128)(2,1)S(1)}, bf16[16,128,128]{2,1,0:T(8,128)(2,1)S(1)}, u32[]{:S(2)}, u32[]{:S(2)}) collective-permute-start(bf16[16,128,128]{2,1,0:T(8,128)(2,1)S(1)} %combine.1.x_ref), channel_id=1, source_target_pairs={{0,1},{1,0},{2,3},{3,2},{4,5},{5,4},{6,7},{7,6},{8,9},{9,8},{10,11... | collective-permute-start | bytes 1572872 | tf_op jit(solution)/shard_map/swap_attended/ppermute | solution.py:52
  (21 other events, 112.3 us)

commit v2 on v0

v2 whole, which is shorter than its diff:
```python
import functools

import jax
import jax.numpy as jnp
from jax import lax
from jax.experimental import pallas as pl
from jax.experimental.pallas import tpu as pltpu
from jax.sharding import PartitionSpec as P

QH = 32
KVH = 4
HD = 128
BLK = 128
MAXBLK = 4
STEPS = 4
OWN_MAX = 2
CORES = 2
LOCAL_KV = KVH // CORES
GROUP = QH // KVH
ROWS = GROUP * STEPS
LOCAL_ROWS = LOCAL_KV * ROWS
OWN_ROWS = 2 * LOCAL_KV * STEPS
QROWS = LOCAL_ROWS + OWN_ROWS
STAT_ROWS = 16

norm_eps = 1e-05
masked_score = -1e30
VMEM_LIMIT = 61 * 1024 * 1024
SMALL = pl.CostEstimate(flops=1024, bytes_accessed=1024, transcendentals=0)


class Links:
    def __init__(self, groups, tensor):
        self.groups, self.tensor = groups, tensor
        self.nz = tensor // 4

    def move(self, value, kind, hops=1):
        pairs = []
        for g in range(self.groups):
            for t in range(self.tensor):
                to_g, to_t = g, t
                if kind == "c":
                    to_t = t ^ 1
                elif kind == "y":
                    to_t = t ^ 2
                elif kind == "yc":
                    to_t = t ^ 3
                elif kind == "z":
                    to_t = (t + 4 * hops) % self.tensor
                else:
                    to_g = g ^ 1
                pairs.append((g * self.tensor + t, to_g * self.tensor + to_t))
        return lax.ppermute(value, ("groups", "tensor"), pairs)


def tied(value, others):
    if not others:
        return value
    return lax.optimization_barrier((value,) + tuple(others))[0]


def split_columns(w_kv, core, half):
    rows, width = w_kv.shape
    part = width // (2 * CORES)
    gran = rows // 2

    def kernel(core_ref, half_ref, a, b, c, d, out_a, out_b, out_c, out_d):
        for src, dst in ((a, out_a), (b, out_b), (c, out_c), (d, out_d)):
            dst[...] = src[...]

    whole, halved = pl.BlockSpec((rows, part), lambda j, c, h: (0, j)), pl.BlockSpec(
        (gran, part), lambda j, c, h: (0, j)
    )
    return pl.pallas_call(
        kernel,
        grid_spec=pltpu.PrefetchScalarGridSpec(
            num_scalar_prefetch=2,
            grid=(2,),
            in_specs=[
                pl.BlockSpec((rows, part), lambda j, c, h: (0, CORES * j + c[0])),
                pl.BlockSpec((rows, part), lambda j, c, h: (0, CORES * j + 1 - c[0])),
                pl.BlockSpec((gran, part), lambda j, c, h: (h[0], CORES * j + c[0])),
                pl.BlockSpec((gran, part), lambda j, c, h: (h[0], CORES * j + 1 - c[0])),
            ],
            out_specs=[whole, whole, halved, halved],
        ),
        out_shape=[
            jax.ShapeDtypeStruct((n, 2 * part), w_kv.dtype) for n in (rows, rows, gran, gran)
        ],
        name="split",
    )(core.reshape(1), half.reshape(1), w_kv, w_kv, w_kv, w_kv)


def row_scale(tokens):
    rows, width = tokens.shape
    tile, chunk = 64, 512
    tiles = rows // tile

    def kernel(tok_hbm, out_ref, tok_ref, sems):
        def load(i):
            at = pl.ds(pl.multiple_of(i * tile, tile), tile)
            return pltpu.make_async_copy(tok_hbm.at[at], tok_ref.at[i], sems.at[i])

        for i in range(tiles):
            load(jnp.int32(i)).start()

        @pl.loop(0, tiles)
        def _(i):
            load(i).wait()
            acc = None
            for c in range(0, width, chunk):
                wide = tok_ref[i, :, c : c + chunk].astype(jnp.float32)
                acc = wide * wide if acc is None else acc + wide * wide
            inverse = lax.rsqrt(jnp.sum(acc, axis=1, keepdims=True) / width + norm_eps)
            at = pl.ds(pl.multiple_of(i * tile, tile), tile)
            out_ref[at, :] = jnp.broadcast_to(inverse, (tile, 128))

    return pl.pallas_call(
        kernel,
        in_specs=[pl.BlockSpec(memory_space=pltpu.HBM)],
        out_specs=pl.BlockSpec(memory_space=pltpu.VMEM),
        out_shape=jax.ShapeDtypeStruct((rows, 128), jnp.float32),
        scratch_shapes=[
            pltpu.VMEM((tiles, tile, width), tokens.dtype),
            pltpu.SemaphoreType.DMA((tiles,)),
        ],
        compiler_params=pltpu.CompilerParams(vmem_limit_bytes=VMEM_LIMIT),
        cost_estimate=SMALL,
        name="row_scale",
    )(tokens)


def partial_sum(acc, lhs, gran, scale, gain_ref, offs_ref, base, w_ref, arrived):
    for j, tokens in enumerate(lhs):
        arrived(j)
        lanes = pl.ds(pl.multiple_of(offs_ref[base + j] * gran, gran), gran)
        wide = tokens[...].astype(jnp.float32)
        normed = (wide * scale * gain_ref[:, lanes]).astype(jnp.bfloat16)
        term = jnp.dot(
            normed, w_ref[j * gran : (j + 1) * gran, :], preferred_element_type=jnp.float32
        )
        acc = term if acc is None else acc + term
    return acc


def piece_copies(pieces, gran, w_ref, sems):
    copies, of_granule, at = [], [], 0
    for i, piece in enumerate(pieces):
        rows = piece.shape[0]
        copies.append(pltpu.make_async_copy(piece, w_ref.at[pl.ds(at, rows)], sems.at[i]))
        of_granule += [i if k == 0 else None for k in range(rows // gran)]
        at += rows
    return copies, of_granule


def project(acc, tok, pieces, gran, offs, base):
    own, other, gain, own_scale, other_scale = tok
    rows, width = own.shape
    cols = pieces[0][0].shape[1]
    tile = 384
    tiles = rows // tile
    total = 2 * tiles
    arrays = [a for a, _ in pieces]
    n = sum(a.shape[0] for a in arrays) // gran
    has_acc = acc is not None

    def kernel(offs_ref, *refs):
        refs = list(refs)
        acc_hbm = refs.pop(0) if has_acc else None
        own_hbm, other_hbm, gain_ref, own_scale_ref, other_scale_ref = refs[:5]
        w_hbm, out_hbm = refs[5 : 5 + len(arrays)], refs[5 + len(arrays)]
        lhs_ref, w_ref, in_ref, out_ref, lhs_sem, w_sem, in_sem, out_sem = refs[6 + len(arrays) :]
        w_copies, of_granule = piece_copies(w_hbm, gran, w_ref, w_sem)

        def loads(source, t, i, slot):
            found = []
            for j in range(n):
                lanes = pl.ds(pl.multiple_of(offs_ref[base + j] * gran, gran), gran)
                found.append(
                    pltpu.make_async_copy(
                        source.at[pl.ds(pl.multiple_of(t * tile, tile), tile), lanes],
                        lhs_ref.at[slot, j],
                        lhs_sem.at[slot, j],
                    )
                )
            return found

        def acc_load(i, slot):
            return pltpu.make_async_copy(
                acc_hbm.at[pl.ds(pl.multiple_of(i * tile, tile), tile)],
                in_ref.at[slot],
                in_sem.at[slot],
            )

        def store(i, slot):
            return pltpu.make_async_copy(
                out_ref.at[slot],
                out_hbm.at[pl.ds(pl.multiple_of(i * tile, tile), tile)],
                out_sem.at[slot],
            )

        def start(i, slot):
            @pl.when(i < tiles)
            def _():
                for copy in loads(own_hbm, i, i, slot):
                    copy.start()

            @pl.when((i >= tiles) & (i < total))
            def _():
                for copy in loads(other_hbm, i - tiles, i, slot):
                    copy.start()

            if has_acc:

                @pl.when(i < total)
                def _():
                    acc_load(i, slot).start()

        start(jnp.int32(0), 0)
        for copy in w_copies:
            copy.start()

        @pl.loop(0, total)
        def _(i):
            slot = lax.rem(i, 2)
            start(i + 1, 1 - slot)

            @pl.when(i == 0)
            def _():
                for copy in w_copies:
                    copy.wait()

            for copy in loads(own_hbm, 0, i, slot):
                copy.wait()
            if has_acc:
                acc_load(i, slot).wait()

            @pl.when(i >= 2)
            def _():
                store(i - 2, slot).wait()

            rows_at = pl.ds(pl.multiple_of(lax.rem(i, tiles) * tile, tile), tile)
            scale = jnp.where(i < tiles, own_scale_ref[rows_at, :], other_scale_ref[rows_at, :])
            result = partial_sum(
                in_ref[slot] if has_acc else None,
                [lhs_ref.at[slot, j] for j in range(n)],
                gran,
                scale[:, :1],
                gain_ref,
                offs_ref,
                base,
                w_ref,
                lambda j: None,
            )
            out_ref[slot] = result
            store(i, slot).start()

        for i in (total - 2, total - 1):
            store(jnp.int32(i), i % 2).wait()

    hbm = pl.BlockSpec(memory_space=pltpu.HBM)
    vmem = pl.BlockSpec(memory_space=pltpu.VMEM)
    args = ([acc] if has_acc else []) + [own, other, gain, own_scale, other_scale] + arrays
    return pl.pallas_call(
        kernel,
        in_specs=[pl.BlockSpec(memory_space=pltpu.SMEM)]
        + ([hbm] if has_acc else [])
        + [hbm, hbm, vmem, vmem, vmem]
        + [hbm for _ in arrays],
        out_specs=hbm,
        out_shape=jax.ShapeDtypeStruct((2 * rows, cols), jnp.float32),
        scratch_shapes=[
            pltpu.VMEM((2, n, tile, gran), jnp.bfloat16),
            pltpu.VMEM((n * gran, cols), jnp.bfloat16),
            pltpu.VMEM((2, tile, cols) if has_acc else (1, 8, 128), jnp.float32),
            pltpu.VMEM((2, tile, cols), jnp.float32),
            pltpu.SemaphoreType.DMA((2, n)),
            pltpu.SemaphoreType.DMA((len(arrays),)),
            pltpu.SemaphoreType.DMA((2,)),
            pltpu.SemaphoreType.DMA((2,)),
        ],
        compiler_params=pltpu.CompilerParams(vmem_limit_bytes=VMEM_LIMIT),
        cost_estimate=SMALL,
        name="project",
    )(offs, *args)


def as_row(column):
    n = column.shape[0]
    eye = lax.broadcasted_iota(jnp.int32, (n, n), 0) == lax.broadcasted_iota(jnp.int32, (n, n), 1)
    return jnp.sum(jnp.where(eye, column, 0.0), axis=0, keepdims=True)


def attend_half(kv, base, table_ref, q_ref, out_ref, blocks):
    scale = HD**-0.5
    dims = (((1,), (1,)), ((), ()))
    seen = BLK + OWN_ROWS
    shape = (LOCAL_ROWS, seen)
    col = lax.broadcasted_iota(jnp.int32, shape, 1)
    row = lax.broadcasted_iota(jnp.int32, shape, 0)
    fresh_col = col - BLK - row // ROWS * STEPS
    causal = (fresh_col >= 0) & (fresh_col <= row % STEPS) & (col >= BLK)
    q_head = lax.broadcasted_iota(jnp.int32, (LOCAL_ROWS, HD), 0) // ROWS
    stats = []
    for b in range(blocks):
        slot = table_ref[base + b, 0]
        visible = table_ref[base + b, 1]
        first = table_ref[base + b, 2]
        q = q_ref[slot]
        fresh = q[LOCAL_ROWS:]
        turned = jnp.concatenate([fresh[OWN_ROWS // 2 :], fresh[: OWN_ROWS // 2]], axis=0)
        block = kv[b * BLK : (b + 1) * BLK]
        keys = jnp.concatenate(
            [block[:, : LOCAL_KV * HD], jnp.concatenate([fresh] * LOCAL_KV, axis=1)], axis=0
        )
        wide = jnp.concatenate(
            [jnp.where(q_head == h, q[:LOCAL_ROWS], 0) for h in range(LOCAL_KV)], axis=1
        )
        score = lax.dot_general(wide, keys, dims, preferred_element_type=jnp.float32) * scale
        score = jnp.where((col < visible) | (causal & (first > 0)), score, masked_score)
        top = jnp.max(score, axis=1, keepdims=True)
        grown = jnp.exp(score - top)
        total = jnp.sum(grown, axis=1, keepdims=True)
        probs = grown.astype(jnp.bfloat16)
        values = jnp.concatenate(
            [block[:, LOCAL_KV * HD :], jnp.concatenate([turned] * LOCAL_KV, axis=1)], axis=0
        )
        out = jnp.dot(probs, values, preferred_element_type=jnp.float32) * (1.0 / total)
        for h in range(LOCAL_KV):
            rows = slice(h * ROWS, (h + 1) * ROWS)
            at = b * LOCAL_ROWS + h * ROWS
            out_ref[at : at + ROWS, :] = out[rows, h * HD : (h + 1) * HD].astype(jnp.bfloat16)
        lse = as_row(top + jnp.log(total))
        high = lse.astype(jnp.bfloat16).astype(jnp.float32)
        mid = (lse - high).astype(jnp.bfloat16).astype(jnp.float32)
        low = lse - high - mid
        stats.append(jnp.concatenate([high, mid], axis=1))
        stats.append(jnp.concatenate([low, jnp.zeros_like(low)], axis=1))
    stats.append(jnp.zeros((STAT_ROWS - 2 * blocks, 2 * LOCAL_ROWS), jnp.float32))
    at = blocks * LOCAL_ROWS
    out_ref[at : at + STAT_ROWS, :] = jnp.concatenate(stats, axis=0).astype(jnp.bfloat16)


def attend(acc, tok, pieces, gran, offs, base, table, queries):
    own, other, gain, own_scale, other_scale = tok
    rows, width = own.shape
    cols = acc.shape[1]
    blocks = rows // BLK
    arrays = [a for a, _ in pieces]
    n = sum(a.shape[0] for a in arrays) // gran
    each = queries[0].shape[0]
    out_rows = blocks * LOCAL_ROWS + STAT_ROWS

    def kernel(offs_ref, table_ref, *refs):
        acc_hbm, own_hbm, other_hbm, gain_ref, own_scale_ref, other_scale_ref = refs[:6]
        refs = refs[6:]
        w_hbm, q_hbm, out_ref = refs[: len(arrays)], refs[len(arrays) : -8], refs[-8]
        lhs_ref, w_ref, acc_ref, q_ref, lhs_sem, w_sem, q_sem = refs[-7:]
        w_copies, of_granule = piece_copies(w_hbm, gran, w_ref, w_sem)
        q_copies = [
            pltpu.make_async_copy(q, q_ref.at[pl.ds(i * each, each)], q_sem.at[i])
            for i, q in enumerate(q_hbm)
        ]
        loads = []
        for side, source in enumerate((own_hbm, other_hbm)):
            found = [
                pltpu.make_async_copy(
                    acc_hbm.at[pl.ds(side * rows, rows)], acc_ref.at[side], lhs_sem.at[side, n]
                )
            ]
            for j in range(n):
                lanes = pl.ds(pl.multiple_of(offs_ref[base + j] * gran, gran), gran)
                found.append(
                    pltpu.make_async_copy(
                        source.at[:, lanes], lhs_ref.at[side, j], lhs_sem.at[side, j]
                    )
                )
            loads.append(found)
        for copy in loads[0] + w_copies + q_copies + loads[1]:
            copy.start()
        for side, scale_ref in enumerate((own_scale_ref, other_scale_ref)):
            loads[side][0].wait()

            def arrived(j):
                loads[side][1 + j].wait()
                if side == 0 and of_granule[j] is not None:
                    w_copies[of_granule[j]].wait()

            kv = partial_sum(
                acc_ref[side],
                [lhs_ref.at[side, j] for j in range(n)],
                gran,
                scale_ref[:, :1],
                gain_ref,
                offs_ref,
                base,
                w_ref,
                arrived,
            ).astype(jnp.bfloat16)
            if side == 0:
                for copy in q_copies:
                    copy.wait()
            attend_half(kv, side * blocks, table_ref, q_ref, out_ref.at[side], blocks)

    hbm = pl.BlockSpec(memory_space=pltpu.HBM)
    vmem = pl.BlockSpec(memory_space=pltpu.VMEM)
    smem = pl.BlockSpec(memory_space=pltpu.SMEM)
    return pl.pallas_call(
        kernel,
        in_specs=[smem, smem, hbm, hbm, hbm, vmem, vmem, vmem] + [hbm] * (len(arrays) + len(queries)),
        out_specs=vmem,
        out_shape=jax.ShapeDtypeStruct((2, out_rows, HD), jnp.bfloat16),
        scratch_shapes=[
            pltpu.VMEM((2, n, rows, gran), jnp.bfloat16),
            pltpu.VMEM((n * gran, cols), jnp.bfloat16),
            pltpu.VMEM((2, rows, cols), jnp.float32),
            pltpu.VMEM((each * len(queries), QROWS, HD), jnp.bfloat16),
            pltpu.SemaphoreType.DMA((2, n + 1)),
            pltpu.SemaphoreType.DMA((len(arrays),)),
            pltpu.SemaphoreType.DMA((len(queries),)),
        ],
        compiler_params=pltpu.CompilerParams(vmem_limit_bytes=VMEM_LIMIT),
        cost_estimate=SMALL,
        name="attend",
    )(offs, table, acc, own, other, gain, own_scale, other_scale, *arrays, *queries)


def weight_copies(w_hbm, w_ref, sems, side, heads, group):
    copies = []
    for i, h in enumerate(range(0, heads, group)):
        at = pl.multiple_of(side * heads * HD + h * HD, HD)
        copies.append(
            pltpu.make_async_copy(
                w_hbm.at[pl.ds(at, group * HD)], w_ref.at[pl.ds(h * HD, group * HD)], sems.at[i]
            )
        )
    return copies


def times_weights(x_ref, w_ref, copies, group, total):
    for i, copy in enumerate(copies):
        copy.wait()
        h = i * group
        x = jnp.concatenate([x_ref[h + k] for k in range(group)], axis=1)
        term = jnp.dot(
            x, w_ref[h * HD : (h + group) * HD, :], preferred_element_type=jnp.float32
        )
        total = term if total is None else total + term
    return total


def combine(parts, halves, blocks, slots, entry_slots, w_out, core):
    heads = LOCAL_ROWS // STEPS
    entries = entry_slots.shape[0]
    cols = w_out.shape[1]
    group = 4
    per = 8

    def kernel(core_ref, slot_ref, slot_row_ref, w_hbm, *refs):
        ins = refs[: len(parts)]
        out_ref, product_ref, acc_ref, w_ref, sems = refs[len(parts) :]
        copies = weight_copies(w_hbm, w_ref, sems, core_ref[0], heads, group)
        for copy in copies:
            copy.start()
        acc_ref[...] = jnp.zeros_like(acc_ref)
        rows = []
        for a, j in halves:
            stat = ins[a][j, blocks * LOCAL_ROWS :, :].astype(jnp.float32)
            for b in range(blocks):
                high, low = stat[2 * b : 2 * b + 1], stat[2 * b + 1 : 2 * b + 2]
                rows.append(high[:, :LOCAL_ROWS] + high[:, LOCAL_ROWS:] + low[:, :LOCAL_ROWS])
            rows.append(jnp.full((per - blocks, LOCAL_ROWS), masked_score, jnp.float32))
        lse = jnp.concatenate(rows, axis=0)
        lse = jnp.concatenate([lse, jnp.zeros_like(lse)], axis=1)
        lse = jnp.concatenate(
            [lse[k : k + 128].T[:LOCAL_ROWS] for k in range(0, lse.shape[0], 128)], axis=1
        )
        owner = slot_row_ref[...]
        weight = jnp.zeros_like(lse)
        for s in range(slots):
            mine = owner == s
            here = jnp.where(mine, lse, 2 * masked_score)
            top = jnp.max(here, axis=1, keepdims=True)
            grown = jnp.where(mine, jnp.exp(here - top), 0.0)
            total = jnp.sum(grown, axis=1, keepdims=True)
            weight = jnp.where(mine, grown / jnp.maximum(total, 1e-30), weight)
        for e, (a, j) in enumerate(halves):
            for b in range(blocks):
                at = e * per + b
                slot = slot_ref[at]
                part = ins[a][j, b * LOCAL_ROWS : (b + 1) * LOCAL_ROWS, :].astype(jnp.float32)
                acc_ref[slot] = acc_ref[slot] + part * weight[:, at : at + 1]
        held = []
        for s in range(slots):
            held.append(acc_ref[s].reshape(heads, STEPS, HD))
            if s % 4 == 3:
                out_ref[:, (s - 3) * STEPS : (s + 1) * STEPS, :] = jnp.concatenate(
                    held, axis=1
                ).astype(jnp.bfloat16)
                held = []
        product_ref[...] = times_weights(out_ref, w_ref, copies, group, None)

    vmem = pl.BlockSpec(memory_space=pltpu.VMEM)
    smem = pl.BlockSpec(memory_space=pltpu.SMEM)
    hbm = pl.BlockSpec(memory_space=pltpu.HBM)
    return pl.pallas_call(
        kernel,
        in_specs=[smem, smem, vmem, hbm] + [vmem for _ in parts],
        out_specs=[vmem, vmem],
        out_shape=[
            jax.ShapeDtypeStruct((heads, slots * STEPS, HD), jnp.bfloat16),
            jax.ShapeDtypeStruct((slots * STEPS, cols), jnp.float32),
        ],
        scratch_shapes=[
            pltpu.VMEM((slots, LOCAL_ROWS, HD), jnp.float32),
            pltpu.VMEM((heads * HD, cols), jnp.bfloat16),
            pltpu.SemaphoreType.DMA((heads // group,)),
        ],
        compiler_params=pltpu.CompilerParams(vmem_limit_bytes=24 * 1024 * 1024),
        name="combine",
    )(core.reshape(1), entry_slots, entry_slots.reshape(1, entries), w_out, *parts)


def out_project(product, other, w_out, core, slots):
    heads, rows, _ = other.shape
    cols = w_out.shape[1]
    group = 4

    def kernel(core_ref, product_ref, other_ref, w_hbm, out_ref, w_ref, sems):
        copies = weight_copies(w_hbm, w_ref, sems, 1 - core_ref[0], heads, group)
        for copy in copies:
            copy.start()
        total = times_weights(other_ref, w_ref, copies, group, product_ref[...])
        out_ref[...] = total.reshape(slots, STEPS, cols).astype(jnp.bfloat16)

    vmem = pl.BlockSpec(memory_space=pltpu.VMEM)
    return pl.pallas_call(
        kernel,
        in_specs=[
            pl.BlockSpec(memory_space=pltpu.SMEM),
            vmem,
            vmem,
            pl.BlockSpec(memory_space=pltpu.HBM),
        ],
        out_specs=vmem,
        out_shape=jax.ShapeDtypeStruct((slots, STEPS, cols), jnp.bfloat16),
        scratch_shapes=[
            pltpu.VMEM((heads * HD, cols), jnp.bfloat16),
            pltpu.SemaphoreType.DMA((heads // group,)),
        ],
        compiler_params=pltpu.CompilerParams(vmem_limit_bytes=24 * 1024 * 1024),
        name="out_project",
    )(core.reshape(1), product, other, w_out)


def block_tables(request_owner, lengths, block_table, n_blocks):
    req_count = request_owner.shape[0]
    req_index = jnp.arange(req_count, dtype=jnp.int32)
    earlier = (request_owner[None, :] == request_owner[:, None]) & (
        req_index[None, :] < req_index[:, None]
    )
    slot_of = request_owner * OWN_MAX + jnp.sum(earlier.astype(jnp.int32), axis=1)
    place = jnp.arange(n_blocks, dtype=jnp.int32) % MAXBLK
    slot = jnp.repeat(slot_of, MAXBLK)
    visible = jnp.clip(jnp.repeat(lengths, MAXBLK) - place * BLK, 0, BLK)
    hit = (block_table[None, :] == jnp.arange(n_blocks, dtype=jnp.int32)[:, None]).astype(jnp.int32)
    values = jnp.stack([slot, visible, (place == 0).astype(jnp.int32)], axis=0)
    return jnp.sum(hit[:, None, :] * values[None, :, :], axis=2)


ORDER = [
    "zB3", "yC", "c", "yB0", "zB1", "ex", "qp", "pair", "zC1", "xC0", "xB1", "stat", "zB2",
    "yBz3", "xC1", "inv", "qc", "zC3", "yq", "yBz1", "xB2", "zC2", "yBx1", "xB3", "qq", "xC3",
    "yBz2", "G1", "zq1", "yBx3", "xC2", "yBx2", "zq3", "zq2", "G2",
]
WAITS = {
    "xC0": ["zB3"],
    "zB2": ["yB0", "stat"],
    "yBz3": ["xC0"],
    "inv": ["xB1"],
    "zC3": ["inv"],
    "yBz1": ["zB2"],
    "xB2": ["yBz3"],
    "zC2": ["yq"],
    "yBx1": ["xC1"],
    "xB3": ["yBz1"],
    "yBz2": ["xB2"],
    "zq1": ["yBx1", "G1"],
    "yBx2": ["yBz2"],
    "zq3": ["xC3"],
    "ex": ["c"],
    "qc": ["ex"],
}
CHAIN = True
STAGES = [
    ["mine", "c", "yB0", "zB1", "zB2", "zB3", "yC", "xB1", "xC0", "zC1"],
    ["xB2", "xB3", "yBz1", "yBz3", "yBz2", "yBx1", "zC3", "xC1", "zC2"],
    ["yBx2", "yBx3", "xC3", "xC2"],
]


def ring(nz):
    both = zip(range(1, nz // 2 + 1), range(nz - 1, nz // 2 - 1, -1))
    return list(dict.fromkeys(k for pair in both for k in pair))


def any_order(nz):
    ks = ring(nz)
    order = ["zB1", "yC", "c", "yB0", "ex", "qp", "qc", "stat", "inv", "pair", "xC0", "yq", "qq"]
    order += [f"zB{k}" for k in ks if k != 1]
    for k in ks:
        order += [f"xB{k}", f"zC{k}", f"yBz{k}"]
    order += ["G1"]
    for k in ks:
        order += [f"zq{k}", f"yBx{k}", f"xC{k}"]
    return order + ["G2"]


def any_stages(nz):
    ks = range(1, nz)
    return [
        ["mine", "c", "yB0", "yC", "xC0"] + [f"zB{k}" for k in ks],
        [f"{n}{k}" for k in ks for n in ("xB", "yBz", "zC")],
        [f"{n}{k}" for k in ks for n in ("yBx", "xC")],
    ]


def on_device(
    links, tokens, norm_gain, w_kv, w_out, lengths, request_owner, block_table, dec_query, dec_new
):
    size, nz = links.tensor, links.nz
    me = lax.axis_index("tensor")
    half = lax.axis_index("groups") % 2
    core = me % CORES
    rows = w_kv.shape[0]
    gran = rows // 2
    blocks = tokens.shape[0] // BLK
    n_blocks = block_table.shape[0]
    slots = OWN_MAX * size
    h0, h1 = half, 1 - half

    mine, theirs, mine_half, theirs_half = split_columns(w_kv, core, half)
    got = {}

    def back(k):
        return (me + size - 4 * k) % size

    def queries_here():
        q = dec_query.reshape(OWN_MAX, STEPS, CORES, LOCAL_ROWS // STEPS, HD)
        q = q.transpose(2, 0, 3, 1, 4).reshape(CORES, OWN_MAX, LOCAL_ROWS, HD)
        new = dec_new.reshape(OWN_MAX, STEPS, 2, CORES, LOCAL_KV, HD).transpose(3, 0, 2, 4, 1, 5)
        return jnp.concatenate([q, new.reshape(CORES, OWN_MAX, OWN_ROWS, HD)], axis=2)

    def at(device, halved):
        return device * 2 + halved

    def places(name):
        if name == "mine":
            return [at(me, 0), at(me, 1)]
        if name == "c":
            return [at(me ^ 1, 0), at(me ^ 1, 1)]
        if name == "yB0":
            return [at(me ^ 2, 0), at(me ^ 2, 1)]
        if name == "yC":
            return [at(me ^ 3, h0)]
        if name == "xC0":
            return [at(me ^ 3, h1)]
        there = back(int(name[-1]))
        kind = name[:-1]
        return {
            "zB": [at(there, h0)],
            "xB": [at(there, h1)],
            "yBz": [at(there ^ 2, h0)],
            "yBx": [at(there ^ 2, h1)],
            "zC": [at(there ^ 1, h0), at(there ^ 3, h0)],
            "xC": [at(there ^ 1, h1), at(there ^ 3, h1)],
        }[kind]

    def piece(name):
        return got[name], places(name)

    stages = STAGES if nz == 4 else any_stages(nz)
    where = [[p for n in names for p in places(n)] for names in stages]
    bases = [sum(len(w) for w in where[:i]) for i in range(len(where))]
    offs = jnp.stack([p for w in where for p in w]).astype(jnp.int32)
    got["mine"] = mine
    tables = block_tables(request_owner, lengths, block_table, n_blocks)
    chip = jnp.concatenate(
        [
            lax.dynamic_slice_in_dim(tables, me * blocks, blocks, 0),
            lax.dynamic_slice_in_dim(tables, (me ^ 1) * blocks, blocks, 0),
        ]
    )
    slot = chip[:, 0]
    holder = slot // OWN_MAX
    far = holder // CORES
    q_at = (me // 4 - far // 2) % nz * 2 + ((far ^ (me // CORES)) & 1)
    q_at = (q_at * CORES + ((holder ^ me) & 1)) * OWN_MAX + slot % OWN_MAX
    table = jnp.stack([q_at, chip[:, 1], chip[:, 2]], axis=1)
    devices = [back(k) ^ other for other in (0, 2) for k in range(nz)]
    devices = jnp.stack([d ^ j for d in devices for j in range(2)])
    entry = jnp.take(tables[:, 0].reshape(size, blocks), devices, axis=0)
    entry = jnp.pad(entry, ((0, 0), (0, 8 - blocks)), constant_values=-1).reshape(-1)
    offs, table, entry, ready = lax.optimization_barrier((offs, table, entry, tokens))
    acc = None
    order = ORDER if nz == 4 else any_order(nz)
    chain = []
    for name in order:
        waits = (chain if CHAIN else []) + ([got[w] for w in WAITS.get(name, [])] if nz == 4 else [])
        kind, k = name.rstrip("0123456789"), int(name[-1]) if name[-1].isdigit() else 0
        with jax.named_scope(name):
            if kind == "G":
                pieces = [piece(n) for n in stages[k - 1]]
                pieces[-1] = (tied(pieces[-1][0], waits), pieces[-1][1])
                chain = [pieces[-1][0]]
                acc = got[name] = project(acc, tok, pieces, gran, offs, bases[k - 1])
                continue
            if kind == "stat":
                chain = [tied(ready, waits)]
                scales = got["stat"] = row_scale(chain[0])
                continue
            if kind == "qp":
                q = tied(queries_here(), waits)
                chain = [q]
                q_mine = lax.dynamic_index_in_dim(q, core, 0, keepdims=False)
                q_other = lax.dynamic_index_in_dim(q, 1 - core, 0, keepdims=False)
                continue
            if kind == "pair":
                c_half = lax.dynamic_slice_in_dim(got["c"], half * gran, gran, 0)
                chain = [tied(c_half, waits)]
                got["pair"] = jnp.concatenate([chain[0], got["yC"]], 0)
                continue
            if kind == "qq":
                got["qq"] = jnp.concatenate([chip_q, tied(got["yq"], waits)])
                continue
            if kind == "yq":
                chip_q = jnp.concatenate([q_mine, got["qc"]])
            hop = 1 if k <= nz // 2 else -1
            before = k - hop
            first = before % nz == 0
            sources = {
                "c": theirs,
                "ex": tokens,
                "inv": None if kind != "inv" else scales,
                "qc": None if kind != "qc" else q_other,
                "yC": theirs_half,
                "yB": mine,
                "zB": mine_half if first else got.get(f"zB{before}"),
                "xB": got.get(f"zB{k}"),
                "yBz": got.get(f"zB{k}"),
                "yBx": got.get(f"xB{k}"),
                "zC": got.get("pair") if first else got.get(f"zC{before}"),
                "xC": got.get(f"zC{k}") if k else got.get("yC"),
                "zq": got.get("qq") if first else got.get(f"zq{before}"),
                "yq": None if kind != "yq" else chip_q,
            }
            along = {"c": "c", "ex": "c", "inv": "c", "qc": "c", "yC": "yc"}.get(kind, kind[0])
            chain = [tied(sources[kind], waits)]
            got[name] = links.move(chain[0], along, hop)
        if kind == "inv":
            tok = (tokens, got["ex"], norm_gain.reshape(1, -1), scales, got["inv"])

    queries = [got["qq"]] + [got[f"zq{k}"] for k in range(1, nz)]

    outs = attend(
        acc, tok, [piece(n) for n in stages[-1]], gran, offs, bases[-1], table, queries
    )

    z_got, y_got = {0: outs}, {}
    for k in ring(nz):
        hop = 1 if k <= nz // 2 else -1
        with jax.named_scope(f"oz{k}"):
            z_got[k] = links.move(z_got[(k - hop) % nz], "z", hop)
    for k in [0] + ring(nz):
        with jax.named_scope(f"oy{k}"):
            early = [y_got[0]] if k == 1 else []
            y_got[k] = links.move(tied(z_got[k], early), "y")
    parts = [got_from[k] for got_from in (z_got, y_got) for k in range(nz)]
    halves = [(i, j) for i in range(len(parts)) for j in range(2)]
    attended, product = combine(parts, halves, blocks, slots, entry, w_out, core)
    with jax.named_scope("swap_attended"):
        attended_other = links.move(attended, "c")
    return out_project(product, attended_other, w_out, core, slots)


def solution(mesh):
    placed = (
        P(("groups", "tensor"), None),
        P(),
        P("tensor", None),
        P(None, "tensor"),
        P("groups"),
        P("groups"),
        P("groups"),
        P(("groups", "tensor"), None, None),
        P(("groups", "tensor"), None, None),
    )
    links = Links(mesh.shape["groups"], mesh.shape["tensor"])
    return jax.shard_map(
        functools.partial(on_device, links),
        mesh=mesh,
        in_specs=placed,
        out_specs=P("groups", None, "tensor"),
        check_vma=False,
    )
```

time: 384 us -> 144 us (0.38); the launches traced: 377 us -> 144 us
  waiting for transfers between devices: 241 us -> 41.5 us
  Pallas kernels: 0 us -> 50.5 us
  local copies, waits for them, and re-layouts: 54.2 us -> 9.14 us
  other arithmetic: 30.2 us -> 0.62 us
  starting transfers between devices: 13.9 us -> 41.3 us
  matrix products: 23.5 us -> 0 us
  between operations: 14 us -> 0.8 us
    all_gather x2 -> x0, waiting for transfers between devices: 169 us -> none  [the longest x1 125 us: on_device(): lax.all_gather(w_kv, 'tensor', axis=0, tiled=True)]
    all_to_all x2 -> x0, waiting for transfers between devices: 71.4 us -> none  [the longest x1 40.2 us: on_device(): lax.all_to_all(outgoing, 'tensor', split_axis=0, concat_axis=2, tiled=True)]
    pallas_call x0 -> x7, Pallas kernels: none -> 50.5 us  [the longest x2 24.6 us: project(): pl.pallas_call(kernel, in_specs=[pl.BlockSpec(memory_space=pltpu.SMEM)] +...]
    ppermute x0 -> x37, waiting for transfers between devices: none -> 41.5 us  [move(): return lax.ppermute(value, ('groups', 'tensor'), pairs)]
    ppermute x0 -> x37, starting transfers between devices: none -> 41.3 us  [move(): return lax.ppermute(value, ('groups', 'tensor'), pairs)]
    reshape x6 -> x4, local copies, waits for them, and re-layouts: 24.3 us -> 0.27 us  [the longest x1 0.09 us: block_tables(): visible = jnp.clip(jnp.repeat(lengths, MAXBLK) - place * BLK, 0, BLK)]
    dot_general x6 -> x0, matrix products: 23.5 us -> none  [the longest x1 18.3 us: on_device(): jnp.dot(normed, lax.all_gather(w_kv, 'tensor', axis=0, tiled=True), prefe...]
    all_to_all x2 -> x0, other arithmetic: 22.1 us -> none  [on_device(): lax.all_to_all(spread, 'tensor', split_axis=0, concat_axis=1, tiled=True)]
  transfers between devices with their start and end apart: 4 -> 37, of which waited for: 4 -> 15; matrix products, arithmetic and copies ran while one was open for 2% -> 3% of each run, Pallas kernels for 0% -> 21%
where the time goes in v2:
time: 144 us
  Pallas kernels  50.5 us (35%)
  waiting for transfers between devices  41.5 us (29%)
  starting transfers between devices  41.3 us (29%)
  local copies, waits for them, and re-layouts  9.14 us (6%)
    ppermute x37, waiting for transfers between devices, move(): return lax.ppermute(value, ('groups', 'tensor'), pairs)  41.5 us
    ppermute x37, starting transfers between devices, move(): return lax.ppermute(value, ('groups', 'tensor'), pairs)  41.3 us
    pallas_call x2, Pallas kernels, project(): pl.pallas_call(kernel, in_specs=[pl.BlockSpec(memory_space=pltpu.SMEM)] +...  24.6 us
    pallas_call x1, Pallas kernels, attend(): pl.pallas_call(kernel, in_specs=[smem, smem, hbm, hbm, hbm, vmem, vmem, v...  11.4 us
    pallas_call x1, Pallas kernels, row_scale(): pl.pallas_call(kernel, in_specs=[pl.BlockSpec(memory_space=pltpu.HBM)], o...  5.71 us
    unnamed x53, local copies, waits for them, and re-layouts  5.51 us
    pallas_call x1, Pallas kernels, combine(): pl.pallas_call(kernel, in_specs=[smem, smem, vmem, hbm] + [vmem for _ in...  4.94 us
  transfers between devices with their start and end apart: 37, of which 15 were waited for; matrix products, arithmetic and copies ran while one was open for 3% of the time, Pallas kernels for 21%

profile of v2, /device:TPU:0, one launch (start us, length us, event | category | flops | bytes accessed | tf_op | source)
XLA Modules:
  0.0 143.8 jit_solution(10530588798872382799)
XLA Ops:
  0.0 2.5 %split.1 = (bf16[512,512]{1,0:T(8,128)(2,1)}, bf16[512,512]{1,0:T(8,128)(2,1)}, bf16[256,512]{1,0:T(8,128)(2,1)}, bf16[256,512]{1,0:T(8,128)(2,1)}) custom-call(s32[1]{0:T(128)} %bitcast.core_ref, s32[1]{0:T(128)} %bitcast.67.half_ref, bf16[512,1024]{1,0:T(8,128)(2,1)} %d.1, bf16[512,1024]{1,0:T(8,128)(2,1)} %d.1, bf16[512,1024]{1,0:T(8,128)(2,1)} %d.1, ...), custom_call_target="tpu_custom_call" | custom-call | tf_op jit(solution)/shard_map/split/pallas_call | solution.py:74
  3.0 1.7 %collective-permute-done.refs_6_ = bf16[512,512]{1,0:T(8,128)(2,1)S(1)} collective-permute-done((bf16[512,512]{1,0:T(8,128)(2,1)}, bf16[512,512]{1,0:T(8,128)(2,1)S(1)}, u32[]{:S(2)}, u32[]{:S(2)}) %collective-permute-start) | collective-permute-done | bytes 524320 | tf_op jit(solution)/shard_map/c/ppermute | solution.py:53
  5.2 2.6 %collective-permute-start.3 = (bf16[256,512]{1,0:T(8,128)(2,1)}, bf16[256,512]{1,0:T(8,128)(2,1)S(1)}, u32[]{:S(2)}, u32[]{:S(2)}) collective-permute-start(bf16[256,512]{1,0:T(8,128)(2,1)} %get-tuple-element.57), channel_id=1, source_target_pairs={{0,3},{1,2},{2,1},{3,0},{4,7},{5,6},{6,5},{7,4},{8,11},{9,10},{10,... | collective-permute-start | bytes 786440 | tf_op jit(solution)/shard_map/yC/ppermute | solution.py:53
  7.8 3.6 %collective-permute-start.4 = (bf16[256,512]{1,0:T(8,128)(2,1)}, bf16[256,512]{1,0:T(8,128)(2,1)S(1)}, u32[]{:S(2)}, u32[]{:S(2)}) collective-permute-start(bf16[256,512]{1,0:T(8,128)(2,1)} %get-tuple-element.60), channel_id=1, source_target_pairs={{0,12},{1,13},{2,14},{3,15},{4,0},{5,1},{6,2},{7,3},{8,4},{9,5},{1... | collective-permute-start | bytes 786440 | tf_op jit(solution)/shard_map/zB3/ppermute | solution.py:53
  14.1 0.7 constant_dynamic-update-slice_fusion.1
  14.8 0.8 constant_dynamic-update-slice_fusion
  15.6 1.5 %collective-permute-start.5 = (bf16[512,512]{1,0:T(8,128)(2,1)}, bf16[512,512]{1,0:T(8,128)(2,1)S(1)}, u32[]{:S(2)}, u32[]{:S(2)}) collective-permute-start(bf16[512,512]{1,0:T(8,128)(2,1)} %constant_dynamic-update-slice_fusion), channel_id=1, source_target_pairs={{0,4},{1,5},{2,6},{3,7},{4,8},{5,9},{6,10},{7,11},{8,12},{9,13},{1... | collective-permute-start | bytes 1572872 | tf_op jit(solution)/shard_map/zC1/ppermute | solution.py:53
  18.4 1.4 collective-permute-start.7
  19.8 5.1 %collective-permute-done.2.refs_8_ = bf16[256,512]{1,0:T(8,128)(2,1)} collective-permute-done((bf16[256,512]{1,0:T(8,128)(2,1)}, bf16[256,512]{1,0:T(8,128)(2,1)}, u32[]{:S(2)}, u32[]{:S(2)}) %collective-permute-start.2) | collective-permute-done | bytes 262176 | tf_op jit(solution)/shard_map/zB1/ppermute | solution.py:53
  24.9 1.4 collective-permute-start.8
  26.3 5.7 %row_scale.1.refs_3_.refs_4_ = f32[768,128]{1,0:T(8,128)} custom-call(bf16[768,8192]{1,0:T(8,128)(2,1)} %refs_1_.3), custom_call_target="tpu_custom_call" | custom-call | flops 1024 | bytes 1024 | tf_op jit(solution)/shard_map/stat/row_scale/pallas_call | solution.py:118
  32.1 3.1 %collective-permute-done.5.refs_14_ = bf16[512,512]{1,0:T(8,128)(2,1)S(1)} collective-permute-done((bf16[512,512]{1,0:T(8,128)(2,1)}, bf16[512,512]{1,0:T(8,128)(2,1)S(1)}, u32[]{:S(2)}, u32[]{:S(2)}) %collective-permute-start.5) | collective-permute-done | bytes 524320 | tf_op jit(solution)/shard_map/zC1/ppermute | solution.py:53
  35.3 1.7 %collective-permute-start.10 = (bf16[256,512]{1,0:T(8,128)(2,1)}, bf16[256,512]{1,0:T(8,128)(2,1)}, u32[]{:S(2)}, u32[]{:S(2)}) collective-permute-start(bf16[256,512]{1,0:T(8,128)(2,1)} %collective-permute-done.2.refs_8_), channel_id=1, source_target_pairs={{0,4},{1,5},{2,6},{3,7},{4,8},{5,9},{6,10},{7,11},{8,12},{9,13},{1... | collective-permute-start | bytes 786440 | tf_op jit(solution)/shard_map/zB2/ppermute | solution.py:53
  37.5 1.4 collective-permute-start.15
  39.0 2.3 %collective-permute-start.11 = (bf16[512,512]{1,0:T(8,128)(2,1)}, bf16[512,512]{1,0:T(8,128)(2,1)S(1)}, u32[]{:S(2)}, u32[]{:S(2)}) collective-permute-start(bf16[512,512]{1,0:T(8,128)(2,1)} %constant_dynamic-update-slice_fusion), channel_id=1, source_target_pairs={{0,12},{1,13},{2,14},{3,15},{4,0},{5,1},{6,2},{7,3},{8,4},{9,5},{1... | collective-permute-start | bytes 1572872 | tf_op jit(solution)/shard_map/zC3/ppermute | solution.py:53
  41.3 1.6 %collective-permute-start.14 = (bf16[4,80,128]{2,1,0:T(8,128)(2,1)S(1)}, bf16[4,80,128]{2,1,0:T(8,128)(2,1)S(1)}, u32[]{:S(2)}, u32[]{:S(2)}) collective-permute-start(bf16[4,80,128]{2,1,0:T(8,128)(2,1)S(1)} %pad_maximum_fusion.2), channel_id=1, source_target_pairs={{0,2},{1,3},{2,0},{3,1},{4,6},{5,7},{6,4},{7,5},{8,10},{9,11},{10,... | collective-permute-start | bytes 245768 | tf_op jit(solution)/shard_map/yq/ppermute | solution.py:53
  42.9 3.8 %collective-permute-done.10.refs_9_ = bf16[256,512]{1,0:T(8,128)(2,1)} collective-permute-done((bf16[256,512]{1,0:T(8,128)(2,1)}, bf16[256,512]{1,0:T(8,128)(2,1)}, u32[]{:S(2)}, u32[]{:S(2)}) %collective-permute-start.10) | collective-permute-done | bytes 262176 | tf_op jit(solution)/shard_map/zB2/ppermute | solution.py:53
  47.4 1.4 collective-permute-start.17
  48.8 3.5 %collective-permute-done.15.refs_13_ = bf16[512,512]{1,0:T(8,128)(2,1)S(1)} collective-permute-done((bf16[512,512]{1,0:T(8,128)(2,1)S(1)}, bf16[512,512]{1,0:T(8,128)(2,1)S(1)}, u32[]{:S(2)}, u32[]{:S(2)}) %collective-permute-start.15) | collective-permute-done | bytes 524320 | tf_op jit(solution)/shard_map/xC1/ppermute | solution.py:53
  52.3 1.5 %collective-permute-start.20 = (bf16[256,512]{1,0:T(8,128)(2,1)}, bf16[256,512]{1,0:T(8,128)(2,1)}, u32[]{:S(2)}, u32[]{:S(2)}) collective-permute-start(bf16[256,512]{1,0:T(8,128)(2,1)} %collective-permute-done.8.refs_12_), channel_id=1, source_target_pairs={{0,2},{1,3},{2,0},{3,1},{4,6},{5,7},{6,4},{7,5},{8,10},{9,11},{10,... | collective-permute-start | bytes 786440 | tf_op jit(solution)/shard_map/yBx1/ppermute | solution.py:53
  53.9 1.6 %collective-permute-done.16.refs_8_ = bf16[256,512]{1,0:T(8,128)(2,1)S(1)} collective-permute-done((bf16[256,512]{1,0:T(8,128)(2,1)}, bf16[256,512]{1,0:T(8,128)(2,1)S(1)}, u32[]{:S(2)}, u32[]{:S(2)}) %collective-permute-start.16) | collective-permute-done | bytes 262176 | tf_op jit(solution)/shard_map/yBz1/ppermute | solution.py:53
  55.5 1.4 collective-permute-start.18
  56.8 1.0 collective-permute-done.11.refs_12_
  57.8 1.3 collective-permute-start.23
  59.8 12.5 %project.2.refs_0_ = f32[1536,512]{1,0:T(8,128)} custom-call(s32[32]{0:T(128)} %stack.226.offs_ref, bf16[768,8192]{1,0:T(8,128)(2,1)} %refs_1_.3, bf16[768,8192]{1,0:T(8,128)(2,1)} %collective-permute-done.1.refs_1_.refs_2_, f32[1,8192]{1,0:T(1,128)} %bitcast.79, f32[768,128]{1,0:T(8,128)} %row_scale.1.refs_3_.refs_4_, f32[768,128]{1,0:T(8,128)} %copy-done.3, ...), custom_call_target="tpu_custom_call" | custom-call | flops 1024 | bytes 1024 | tf_op jit(solution)/shard_map/G1/project/pallas_call | solution.py:264
  72.4 1.2 collective-permute-start.26
  73.6 1.4 collective-permute-start.25
  75.7 5.1 %collective-permute-done.22.refs_11_ = bf16[8,80,128]{2,1,0:T(8,128)(2,1)S(1)} collective-permute-done((bf16[8,80,128]{2,1,0:T(8,128)(2,1)S(1)}, bf16[8,80,128]{2,1,0:T(8,128)(2,1)S(1)}, u32[]{:S(2)}, u32[]{:S(2)}) %collective-permute-start.22) | collective-permute-done | bytes 163872 | tf_op jit(solution)/shard_map/zq1/ppermute | solution.py:53
  80.8 3.8 %collective-permute-start.28 = (bf16[8,80,128]{2,1,0:T(8,128)(2,1)S(1)}, bf16[8,80,128]{2,1,0:T(8,128)(2,1)S(1)}, u32[]{:S(2)}, u32[]{:S(2)}) collective-permute-start(bf16[8,80,128]{2,1,0:T(8,128)(2,1)S(1)} %pad_maximum_fusion.refs_10_), channel_id=1, source_target_pairs={{0,12},{1,13},{2,14},{3,15},{4,0},{5,1},{6,2},{7,3},{8,4},{9,5},{1... | collective-permute-start | bytes 491528 | tf_op jit(solution)/shard_map/zq3/ppermute | solution.py:53
  84.6 0.7 copy.19.table_ref
  85.3 12.1 %project.3.refs_0_ = f32[1536,512]{1,0:T(8,128)} custom-call(s32[32]{0:T(128)} %stack.226.offs_ref, f32[1536,512]{1,0:T(8,128)} %project.2.refs_0_, bf16[768,8192]{1,0:T(8,128)(2,1)} %refs_1_.3, bf16[768,8192]{1,0:T(8,128)(2,1)} %collective-permute-done.1.refs_1_.refs_2_, f32[1,8192]{1,0:T(1,128)} %bitcast.80, f32[768,128]{1,0:T(8,128)} %row_scale.1.refs_3_.refs_4_, ...), custom_call_target="tpu_custom_call" | custom-call | flops 1024 | bytes 1024 | tf_op jit(solution)/shard_map/G2/project/pallas_call | solution.py:264
  97.5 0.6 copy-done.16
  98.4 0.7 copy-done.20
  99.1 11.4 %attend.1.refs_0_ = bf16[2,400,128]{2,1,0:T(8,128)(2,1)} custom-call(s32[32]{0:T(128)} %stack.226.offs_ref, s32[12,3]{1,0:T(8,128)} %copy.19.table_ref, f32[1536,512]{1,0:T(8,128)} %project.3.refs_0_, bf16[768,8192]{1,0:T(8,128)(2,1)} %refs_1_.3, bf16[768,8192]{1,0:T(8,128)(2,1)} %collective-permute-done.1.refs_1_.refs_2_, f32[1,8192]{1,0:T(1,128)} %bitcast.81, ...), custom_call_target="tpu_custom_call" | custom-call | flops 1024 | bytes 1024 | tf_op jit(solution)/shard_map/attend/pallas_call | solution.py:408
  110.5 1.1 collective-permute-start.32
  111.6 3.7 %collective-permute-start.31 = (bf16[2,400,128]{2,1,0:T(8,128)(2,1)}, bf16[2,400,128]{2,1,0:T(8,128)(2,1)S(1)}, u32[]{:S(2)}, u32[]{:S(2)}) collective-permute-start(bf16[2,400,128]{2,1,0:T(8,128)(2,1)} %attend.1.refs_0_), channel_id=1, source_target_pairs={{0,12},{1,13},{2,14},{3,15},{4,0},{5,1},{6,2},{7,3},{8,4},{9,5},{1... | collective-permute-start | bytes 614408 | tf_op jit(solution)/shard_map/oz3/ppermute | solution.py:53
  115.4 3.5 %collective-permute-done.29.refs_1_ = bf16[2,400,128]{2,1,0:T(8,128)(2,1)S(1)} collective-permute-done((bf16[2,400,128]{2,1,0:T(8,128)(2,1)}, bf16[2,400,128]{2,1,0:T(8,128)(2,1)S(1)}, u32[]{:S(2)}, u32[]{:S(2)}) %collective-permute-start.29) | collective-permute-done | bytes 204832 | tf_op jit(solution)/shard_map/oz1/ppermute | solution.py:53
  118.9 1.4 collective-permute-start.33
  120.3 1.8 %collective-permute-done.31.refs_3_ = bf16[2,400,128]{2,1,0:T(8,128)(2,1)S(1)} collective-permute-done((bf16[2,400,128]{2,1,0:T(8,128)(2,1)}, bf16[2,400,128]{2,1,0:T(8,128)(2,1)S(1)}, u32[]{:S(2)}, u32[]{:S(2)}) %collective-permute-start.31) | collective-permute-done | bytes 204832 | tf_op jit(solution)/shard_map/oz3/ppermute | solution.py:53
  122.0 4.4 %collective-permute-done.30.refs_2_ = bf16[2,400,128]{2,1,0:T(8,128)(2,1)S(1)} collective-permute-done((bf16[2,400,128]{2,1,0:T(8,128)(2,1)S(1)}, bf16[2,400,128]{2,1,0:T(8,128)(2,1)S(1)}, u32[]{:S(2)}, u32[]{:S(2)}) %collective-permute-start.30) | collective-permute-done | bytes 204832 | tf_op jit(solution)/shard_map/oz2/ppermute | solution.py:53
  126.4 1.4 collective-permute-start.34
  127.8 2.0 %collective-permute-done.35.refs_7_ = bf16[2,400,128]{2,1,0:T(8,128)(2,1)S(1)} collective-permute-done((bf16[2,400,128]{2,1,0:T(8,128)(2,1)S(1)}, bf16[2,400,128]{2,1,0:T(8,128)(2,1)S(1)}, u32[]{:S(2)}, u32[]{:S(2)}) %collective-permute-start.35) | collective-permute-done | bytes 204832 | tf_op jit(solution)/shard_map/oy3/ppermute | solution.py:53
  129.9 2.3 %collective-permute-done.34.refs_6_ = bf16[2,400,128]{2,1,0:T(8,128)(2,1)S(1)} collective-permute-done((bf16[2,400,128]{2,1,0:T(8,128)(2,1)S(1)}, bf16[2,400,128]{2,1,0:T(8,128)(2,1)S(1)}, u32[]{:S(2)}, u32[]{:S(2)}) %collective-permute-start.34) | collective-permute-done | bytes 204832 | tf_op jit(solution)/shard_map/oy2/ppermute | solution.py:53
  132.2 2.2 %copy-done = bf16[4096,512]{1,0:T(8,128)(2,1)S(1)} copy-done((bf16[4096,512]{1,0:T(8,128)(2,1)S(1)}, bf16[4096,512]{1,0:T(8,128)(2,1)}, u32[]{:S(2)}) %copy-start) | copy-done | bytes 4194328
  134.4 0.9 copy-done.2
  135.3 4.9 %combine.1 = (bf16[16,128,128]{2,1,0:T(8,128)(2,1)S(1)}, f32[128,512]{1,0:T(8,128)S(1)}) custom-call(s32[1]{0:T(128)} %bitcast.core_ref, s32[128]{0:T(128)S(1)} %reshape.785.slot_ref, s32[1,128]{1,0:T(1,128)S(1)} %bitcast.78, bf16[4096,512]{1,0:T(8,128)(2,1)S(1)} %copy-done, bf16[2,400,128]{2,1,0:T(8,128)(2,1)S(1)} %copy-done.2, ...), custom_call_target="tpu_custom_call" | custom-call | tf_op jit(solution)/shard_map/combine/pallas_call | solution.py:506
  140.3 1.9 %collective-permute-done.36.other_ref = bf16[16,128,128]{2,1,0:T(8,128)(2,1)S(1)} collective-permute-done((bf16[16,128,128]{2,1,0:T(8,128)(2,1)S(1)}, bf16[16,128,128]{2,1,0:T(8,128)(2,1)S(1)}, u32[]{:S(2)}, u32[]{:S(2)}) %collective-permute-start.36) | collective-permute-done | bytes 524320 | tf_op jit(solution)/shard_map/swap_attended/ppermute | solution.py:53
  142.2 1.5 %out_project.1 = bf16[32,4,512]{2,1,0:T(4,128)(2,1)} custom-call(s32[1]{0:T(128)} %bitcast.core_ref, f32[128,512]{1,0:T(8,128)S(1)} %get-tuple-element.93.product_ref, bf16[16,128,128]{2,1,0:T(8,128)(2,1)S(1)} %collective-permute-done.36.other_ref, bf16[4096,512]{1,0:T(8,128)(2,1)S(1)} %copy-done.1), custom_call_target="tpu_custom_call" | custom-call | tf_op jit(solution)/shard_map/out_project/pallas_call | solution.py:537
  (125 shorter events, 8.0 us)
Async XLA Ops:
  0.0 12.7 %copy-start.23 = (s32[96]{0:T(128)S(1)}, s32[96]{0:T(128)}, u32[]{:S(2)}) copy-start(s32[96]{0:T(128)} %param.15) | copy-start | bytes 1156
  2.5 2.2 %collective-permute-start = (bf16[512,512]{1,0:T(8,128)(2,1)}, bf16[512,512]{1,0:T(8,128)(2,1)S(1)}, u32[]{:S(2)}, u32[]{:S(2)}) collective-permute-start(bf16[512,512]{1,0:T(8,128)(2,1)} %get-tuple-element.58), channel_id=1, source_target_pairs={{0,1},{1,0},{2,3},{3,2},{4,5},{5,4},{6,7},{7,6},{8,9},{9,8},{10,11... | collective-permute-start | bytes 1572872 | tf_op jit(solution)/shard_map/c/ppermute | solution.py:53
  4.8 27.3 %copy-start.4 = (bf16[512,512]{1,0:T(8,128)(2,1)}, bf16[512,512]{1,0:T(8,128)(2,1)S(1)}, u32[]{:S(2)}) copy-start(bf16[512,512]{1,0:T(8,128)(2,1)S(1)} %collective-permute-done.refs_6_) | copy-start | bytes 1572868
  4.8 34.1 %collective-permute-start.1 = (bf16[768,8192]{1,0:T(8,128)(2,1)}, bf16[768,8192]{1,0:T(8,128)(2,1)}, u32[]{:S(2)}, u32[]{:S(2)}) collective-permute-start(bf16[768,8192]{1,0:T(8,128)(2,1)} %refs_1_.3), channel_id=1, source_target_pairs={{0,1},{1,0},{2,3},{3,2},{4,5},{5,4},{6,7},{7,6},{8,9},{9,8},{10,11... | collective-permute-start | bytes 37748744 | tf_op jit(solution)/shard_map/ex/ppermute | solution.py:53
  5.2 9.7 %collective-permute-start.3 = (bf16[256,512]{1,0:T(8,128)(2,1)}, bf16[256,512]{1,0:T(8,128)(2,1)S(1)}, u32[]{:S(2)}, u32[]{:S(2)}) collective-permute-start(bf16[256,512]{1,0:T(8,128)(2,1)} %get-tuple-element.57), channel_id=1, source_target_pairs={{0,3},{1,2},{2,1},{3,0},{4,7},{5,6},{6,5},{7,4},{8,11},{9,10},{10,... | collective-permute-start | bytes 786440 | tf_op jit(solution)/shard_map/yC/ppermute | solution.py:53
  7.8 10.6 %collective-permute-start.4 = (bf16[256,512]{1,0:T(8,128)(2,1)}, bf16[256,512]{1,0:T(8,128)(2,1)S(1)}, u32[]{:S(2)}, u32[]{:S(2)}) collective-permute-start(bf16[256,512]{1,0:T(8,128)(2,1)} %get-tuple-element.60), channel_id=1, source_target_pairs={{0,12},{1,13},{2,14},{3,15},{4,0},{5,1},{6,2},{7,3},{8,4},{9,5},{1... | collective-permute-start | bytes 786440 | tf_op jit(solution)/shard_map/zB3/ppermute | solution.py:53
  11.4 13.5 %collective-permute-start.2 = (bf16[256,512]{1,0:T(8,128)(2,1)}, bf16[256,512]{1,0:T(8,128)(2,1)}, u32[]{:S(2)}, u32[]{:S(2)}) collective-permute-start(bf16[256,512]{1,0:T(8,128)(2,1)} %get-tuple-element.60), channel_id=1, source_target_pairs={{0,4},{1,5},{2,6},{3,7},{4,8},{5,9},{6,10},{7,11},{8,12},{9,13},{1... | collective-permute-start | bytes 786440 | tf_op jit(solution)/shard_map/zB1/ppermute | solution.py:53
  11.4 20.7 %collective-permute-start.6 = (bf16[512,512]{1,0:T(8,128)(2,1)}, bf16[512,512]{1,0:T(8,128)(2,1)S(1)}, u32[]{:S(2)}, u32[]{:S(2)}) collective-permute-start(bf16[512,512]{1,0:T(8,128)(2,1)} %get-tuple-element.59.refs_5_), channel_id=1, source_target_pairs={{0,2},{1,3},{2,0},{3,1},{4,6},{5,7},{6,4},{7,5},{8,10},{9,11},{10,... | collective-permute-start | bytes 1572872 | tf_op jit(solution)/shard_map/yB0/ppermute | solution.py:53
  14.8 17.2 %copy-start.5 = (bf16[256,512]{1,0:T(8,128)(2,1)}, bf16[256,512]{1,0:T(8,128)(2,1)S(1)}, u32[]{:S(2)}) copy-start(bf16[256,512]{1,0:T(8,128)(2,1)S(1)} %collective-permute-done.3.refs_11_) | copy-start | bytes 786436
  15.6 19.6 %collective-permute-start.5 = (bf16[512,512]{1,0:T(8,128)(2,1)}, bf16[512,512]{1,0:T(8,128)(2,1)S(1)}, u32[]{:S(2)}, u32[]{:S(2)}) collective-permute-start(bf16[512,512]{1,0:T(8,128)(2,1)} %constant_dynamic-update-slice_fusion), channel_id=1, source_target_pairs={{0,4},{1,5},{2,6},{3,7},{4,8},{5,9},{6,10},{7,11},{8,12},{9,13},{1... | collective-permute-start | bytes 1572872 | tf_op jit(solution)/shard_map/zC1/ppermute | solution.py:53
  18.4 37.0 %copy-start.12 = (bf16[256,512]{1,0:T(8,128)(2,1)}, bf16[256,512]{1,0:T(8,128)(2,1)S(1)}, u32[]{:S(2)}) copy-start(bf16[256,512]{1,0:T(8,128)(2,1)S(1)} %collective-permute-done.4.refs_10_) | copy-start | bytes 786436
  18.4 13.7 %collective-permute-start.7 = (bf16[256,512]{1,0:T(8,128)(2,1)S(1)}, bf16[256,512]{1,0:T(8,128)(2,1)S(1)}, u32[]{:S(2)}, u32[]{:S(2)}) collective-permute-start(bf16[256,512]{1,0:T(8,128)(2,1)S(1)} %collective-permute-done.3.refs_11_), channel_id=1, source_target_pairs={{0,16},{1,17},{2,18},{3,19},{4,20},{5,21},{6,22},{7,23},{8,24},{9,... | collective-permute-start | bytes 786440 | tf_op jit(solution)/shard_map/xC0/ppermute | solution.py:53
  24.9 10.3 %collective-permute-start.8 = (bf16[256,512]{1,0:T(8,128)(2,1)}, bf16[256,512]{1,0:T(8,128)(2,1)}, u32[]{:S(2)}, u32[]{:S(2)}) collective-permute-start(bf16[256,512]{1,0:T(8,128)(2,1)} %collective-permute-done.2.refs_8_), channel_id=1, source_target_pairs={{0,16},{1,17},{2,18},{3,19},{4,20},{5,21},{6,22},{7,23},{8,24},{9,... | collective-permute-start | bytes 786440 | tf_op jit(solution)/shard_map/xB1/ppermute | solution.py:53
  32.1 27.7 %copy-start.7 = (bf16[512,512]{1,0:T(8,128)(2,1)}, bf16[512,512]{1,0:T(8,128)(2,1)S(1)}, u32[]{:S(2)}) copy-start(bf16[512,512]{1,0:T(8,128)(2,1)S(1)} %collective-permute-done.6.refs_7_) | copy-start | bytes 1572868
  35.2 24.6 %copy-start.8 = (bf16[512,512]{1,0:T(8,128)(2,1)}, bf16[512,512]{1,0:T(8,128)(2,1)S(1)}, u32[]{:S(2)}) copy-start(bf16[512,512]{1,0:T(8,128)(2,1)S(1)} %collective-permute-done.5.refs_14_) | copy-start | bytes 1572868
  35.2 3.7 %collective-permute-start.9 = (f32[768,128]{1,0:T(8,128)}, f32[768,128]{1,0:T(8,128)S(1)}, u32[]{:S(2)}, u32[]{:S(2)}) collective-permute-start(f32[768,128]{1,0:T(8,128)} %row_scale.1.refs_3_.refs_4_), channel_id=1, source_target_pairs={{0,1},{1,0},{2,3},{3,2},{4,5},{5,4},{6,7},{7,6},{8,9},{9,8},{10,11... | collective-permute-start | bytes 1179656 | tf_op jit(solution)/shard_map/inv/ppermute | solution.py:53
  35.3 11.3 %collective-permute-start.10 = (bf16[256,512]{1,0:T(8,128)(2,1)}, bf16[256,512]{1,0:T(8,128)(2,1)}, u32[]{:S(2)}, u32[]{:S(2)}) collective-permute-start(bf16[256,512]{1,0:T(8,128)(2,1)} %collective-permute-done.2.refs_8_), channel_id=1, source_target_pairs={{0,4},{1,5},{2,6},{3,7},{4,8},{5,9},{6,10},{7,11},{8,12},{9,13},{1... | collective-permute-start | bytes 786440 | tf_op jit(solution)/shard_map/zB2/ppermute | solution.py:53
  37.0 10.2 %collective-permute-start.13 = (bf16[256,512]{1,0:T(8,128)(2,1)S(1)}, bf16[256,512]{1,0:T(8,128)(2,1)S(1)}, u32[]{:S(2)}, u32[]{:S(2)}) collective-permute-start(bf16[256,512]{1,0:T(8,128)(2,1)S(1)} %collective-permute-done.4.refs_10_), channel_id=1, source_target_pairs={{0,2},{1,3},{2,0},{3,1},{4,6},{5,7},{6,4},{7,5},{8,10},{9,11},{10,... | collective-permute-start | bytes 786440 | tf_op jit(solution)/shard_map/yBz3/ppermute | solution.py:53
  37.5 14.8 %collective-permute-start.15 = (bf16[512,512]{1,0:T(8,128)(2,1)S(1)}, bf16[512,512]{1,0:T(8,128)(2,1)S(1)}, u32[]{:S(2)}, u32[]{:S(2)}) collective-permute-start(bf16[512,512]{1,0:T(8,128)(2,1)S(1)} %collective-permute-done.5.refs_14_), channel_id=1, source_target_pairs={{0,16},{1,17},{2,18},{3,19},{4,20},{5,21},{6,22},{7,23},{8,24},{9,... | collective-permute-start | bytes 1572872 | tf_op jit(solution)/shard_map/xC1/ppermute | solution.py:53
  38.9 2.4 %collective-permute-start.12 = (bf16[2,80,128]{2,1,0:T(8,128)(2,1)S(1)}, bf16[2,80,128]{2,1,0:T(8,128)(2,1)S(1)}, u32[]{:S(2)}, u32[]{:S(2)}) collective-permute-start(bf16[2,80,128]{2,1,0:T(8,128)(2,1)S(1)} %get-tuple-element.73), channel_id=1, source_target_pairs={{0,1},{1,0},{2,3},{3,2},{4,5},{5,4},{6,7},{7,6},{8,9},{9,8},{10,11... | collective-permute-start | bytes 122888 | tf_op jit(solution)/shard_map/qc/ppermute | solution.py:53
  39.0 20.8 %copy-start.3 = (f32[768,128]{1,0:T(8,128)}, f32[768,128]{1,0:T(8,128)S(1)}, u32[]{:S(2)}) copy-start(f32[768,128]{1,0:T(8,128)S(1)} %collective-permute-done.9.refs_4_.refs_5_) | copy-start | bytes 1179652
  39.0 18.8 %collective-permute-start.11 = (bf16[512,512]{1,0:T(8,128)(2,1)}, bf16[512,512]{1,0:T(8,128)(2,1)S(1)}, u32[]{:S(2)}, u32[]{:S(2)}) collective-permute-start(bf16[512,512]{1,0:T(8,128)(2,1)} %constant_dynamic-update-slice_fusion), channel_id=1, source_target_pairs={{0,12},{1,13},{2,14},{3,15},{4,0},{5,1},{6,2},{7,3},{8,4},{9,5},{1... | collective-permute-start | bytes 1572872 | tf_op jit(solution)/shard_map/zC3/ppermute | solution.py:53
  41.3 5.9 %collective-permute-start.14 = (bf16[4,80,128]{2,1,0:T(8,128)(2,1)S(1)}, bf16[4,80,128]{2,1,0:T(8,128)(2,1)S(1)}, u32[]{:S(2)}, u32[]{:S(2)}) collective-permute-start(bf16[4,80,128]{2,1,0:T(8,128)(2,1)S(1)} %pad_maximum_fusion.2), channel_id=1, source_target_pairs={{0,2},{1,3},{2,0},{3,1},{4,6},{5,7},{6,4},{7,5},{8,10},{9,11},{10,... | collective-permute-start | bytes 245768 | tf_op jit(solution)/shard_map/yq/ppermute | solution.py:53
  46.7 8.8 %collective-permute-start.16 = (bf16[256,512]{1,0:T(8,128)(2,1)}, bf16[256,512]{1,0:T(8,128)(2,1)S(1)}, u32[]{:S(2)}, u32[]{:S(2)}) collective-permute-start(bf16[256,512]{1,0:T(8,128)(2,1)} %collective-permute-done.2.refs_8_), channel_id=1, source_target_pairs={{0,2},{1,3},{2,0},{3,1},{4,6},{5,7},{6,4},{7,5},{8,10},{9,11},{10,... | collective-permute-start | bytes 786440 | tf_op jit(solution)/shard_map/yBz1/ppermute | solution.py:53
  47.2 25.2 %collective-permute-start.21 = (bf16[512,512]{1,0:T(8,128)(2,1)S(1)}, bf16[512,512]{1,0:T(8,128)(2,1)}, u32[]{:S(2)}, u32[]{:S(2)}) collective-permute-start(bf16[512,512]{1,0:T(8,128)(2,1)S(1)} %collective-permute-done.5.refs_14_), channel_id=1, source_target_pairs={{0,4},{1,5},{2,6},{3,7},{4,8},{5,9},{6,10},{7,11},{8,12},{9,13},{1... | collective-permute-start | bytes 1572872 | tf_op jit(solution)/shard_map/zC2/ppermute | solution.py:53
  47.4 11.8 %collective-permute-start.17 = (bf16[256,512]{1,0:T(8,128)(2,1)}, bf16[256,512]{1,0:T(8,128)(2,1)}, u32[]{:S(2)}, u32[]{:S(2)}) collective-permute-start(bf16[256,512]{1,0:T(8,128)(2,1)} %collective-permute-done.10.refs_9_), channel_id=1, source_target_pairs={{0,16},{1,17},{2,18},{3,19},{4,20},{5,21},{6,22},{7,23},{8,24},{9,... | collective-permute-start | bytes 786440 | tf_op jit(solution)/shard_map/xB2/ppermute | solution.py:53
  52.3 20.0 %copy-start.9 = (bf16[512,512]{1,0:T(8,128)(2,1)}, bf16[512,512]{1,0:T(8,128)(2,1)S(1)}, u32[]{:S(2)}) copy-start(bf16[512,512]{1,0:T(8,128)(2,1)S(1)} %collective-permute-done.15.refs_13_) | copy-start | bytes 1572868
  52.3 20.0 %collective-permute-start.20 = (bf16[256,512]{1,0:T(8,128)(2,1)}, bf16[256,512]{1,0:T(8,128)(2,1)}, u32[]{:S(2)}, u32[]{:S(2)}) collective-permute-start(bf16[256,512]{1,0:T(8,128)(2,1)} %collective-permute-done.8.refs_12_), channel_id=1, source_target_pairs={{0,2},{1,3},{2,0},{3,1},{4,6},{5,7},{6,4},{7,5},{8,10},{9,11},{10,... | collective-permute-start | bytes 786440 | tf_op jit(solution)/shard_map/yBx1/ppermute | solution.py:53
  55.5 16.9 %collective-permute-start.18 = (bf16[256,512]{1,0:T(8,128)(2,1)S(1)}, bf16[256,512]{1,0:T(8,128)(2,1)}, u32[]{:S(2)}, u32[]{:S(2)}) collective-permute-start(bf16[256,512]{1,0:T(8,128)(2,1)S(1)} %collective-permute-done.4.refs_10_), channel_id=1, source_target_pairs={{0,16},{1,17},{2,18},{3,19},{4,20},{5,21},{6,22},{7,23},{8,24},{9,... | collective-permute-start | bytes 786440 | tf_op jit(solution)/shard_map/xB3/ppermute | solution.py:53
  57.8 14.5 %copy-start.10 = (bf16[512,512]{1,0:T(8,128)(2,1)}, bf16[512,512]{1,0:T(8,128)(2,1)S(1)}, u32[]{:S(2)}) copy-start(bf16[512,512]{1,0:T(8,128)(2,1)S(1)} %collective-permute-done.11.refs_12_) | copy-start | bytes 1572868
  57.8 17.9 %collective-permute-start.23 = (bf16[512,512]{1,0:T(8,128)(2,1)S(1)}, bf16[512,512]{1,0:T(8,128)(2,1)}, u32[]{:S(2)}, u32[]{:S(2)}) collective-permute-start(bf16[512,512]{1,0:T(8,128)(2,1)S(1)} %collective-permute-done.11.refs_12_), channel_id=1, source_target_pairs={{0,16},{1,17},{2,18},{3,19},{4,20},{5,21},{6,22},{7,23},{8,24},{9,... | collective-permute-start | bytes 1572872 | tf_op jit(solution)/shard_map/xC3/ppermute | solution.py:53
  59.2 21.6 %copy-start.6 = (bf16[8,80,128]{2,1,0:T(8,128)(2,1)}, bf16[8,80,128]{2,1,0:T(8,128)(2,1)S(1)}, u32[]{:S(2)}) copy-start(bf16[8,80,128]{2,1,0:T(8,128)(2,1)S(1)} %pad_maximum_fusion.refs_10_) | copy-start | bytes 491524
  59.2 15.9 %collective-permute-start.19 = (bf16[256,512]{1,0:T(8,128)(2,1)}, bf16[256,512]{1,0:T(8,128)(2,1)}, u32[]{:S(2)}, u32[]{:S(2)}) collective-permute-start(bf16[256,512]{1,0:T(8,128)(2,1)} %collective-permute-done.10.refs_9_), channel_id=1, source_target_pairs={{0,2},{1,3},{2,0},{3,1},{4,6},{5,7},{6,4},{7,5},{8,10},{9,11},{10,... | collective-permute-start | bytes 786440 | tf_op jit(solution)/shard_map/yBz2/ppermute | solution.py:53
  72.4 25.1 %collective-permute-start.26 = (bf16[512,512]{1,0:T(8,128)(2,1)}, bf16[512,512]{1,0:T(8,128)(2,1)S(1)}, u32[]{:S(2)}, u32[]{:S(2)}) collective-permute-start(bf16[512,512]{1,0:T(8,128)(2,1)} %collective-permute-done.21.refs_14_), channel_id=1, source_target_pairs={{0,16},{1,17},{2,18},{3,19},{4,20},{5,21},{6,22},{7,23},{8,24},{9,... | collective-permute-start | bytes 1572872 | tf_op jit(solution)/shard_map/xC2/ppermute | solution.py:53
  73.6 7.2 %collective-permute-start.22 = (bf16[8,80,128]{2,1,0:T(8,128)(2,1)S(1)}, bf16[8,80,128]{2,1,0:T(8,128)(2,1)S(1)}, u32[]{:S(2)}, u32[]{:S(2)}) collective-permute-start(bf16[8,80,128]{2,1,0:T(8,128)(2,1)S(1)} %pad_maximum_fusion.refs_10_), channel_id=1, source_target_pairs={{0,4},{1,5},{2,6},{3,7},{4,8},{5,9},{6,10},{7,11},{8,12},{9,13},{1... | collective-permute-start | bytes 491528 | tf_op jit(solution)/shard_map/zq1/ppermute | solution.py:53
  73.6 23.8 %collective-permute-start.25 = (bf16[256,512]{1,0:T(8,128)(2,1)}, bf16[256,512]{1,0:T(8,128)(2,1)S(1)}, u32[]{:S(2)}, u32[]{:S(2)}) collective-permute-start(bf16[256,512]{1,0:T(8,128)(2,1)} %collective-permute-done.18.refs_7_), channel_id=1, source_target_pairs={{0,2},{1,3},{2,0},{3,1},{4,6},{5,7},{6,4},{7,5},{8,10},{9,11},{10,... | collective-permute-start | bytes 786440 | tf_op jit(solution)/shard_map/yBx3/ppermute | solution.py:53
  75.1 22.4 %collective-permute-start.24 = (bf16[256,512]{1,0:T(8,128)(2,1)}, bf16[256,512]{1,0:T(8,128)(2,1)S(1)}, u32[]{:S(2)}, u32[]{:S(2)}) collective-permute-start(bf16[256,512]{1,0:T(8,128)(2,1)} %collective-permute-done.17.refs_6_), channel_id=1, source_target_pairs={{0,2},{1,3},{2,0},{3,1},{4,6},{5,7},{6,4},{7,5},{8,10},{9,11},{10,... | collective-permute-start | bytes 786440 | tf_op jit(solution)/shard_map/yBx2/ppermute | solution.py:53
  80.8 16.6 %copy-start.18 = (bf16[8,80,128]{2,1,0:T(8,128)(2,1)}, bf16[8,80,128]{2,1,0:T(8,128)(2,1)S(1)}, u32[]{:S(2)}) copy-start(bf16[8,80,128]{2,1,0:T(8,128)(2,1)S(1)} %collective-permute-done.22.refs_11_) | copy-start | bytes 491524
  80.8 16.7 %collective-permute-start.27 = (bf16[8,80,128]{2,1,0:T(8,128)(2,1)S(1)}, bf16[8,80,128]{2,1,0:T(8,128)(2,1)S(1)}, u32[]{:S(2)}, u32[]{:S(2)}) collective-permute-start(bf16[8,80,128]{2,1,0:T(8,128)(2,1)S(1)} %collective-permute-done.22.refs_11_), channel_id=1, source_target_pairs={{0,4},{1,5},{2,6},{3,7},{4,8},{5,9},{6,10},{7,11},{8,12},{9,13},{1... | collective-permute-start | bytes 491528 | tf_op jit(solution)/shard_map/zq2/ppermute | solution.py:53
  80.8 16.7 %collective-permute-start.28 = (bf16[8,80,128]{2,1,0:T(8,128)(2,1)S(1)}, bf16[8,80,128]{2,1,0:T(8,128)(2,1)S(1)}, u32[]{:S(2)}, u32[]{:S(2)}) collective-permute-start(bf16[8,80,128]{2,1,0:T(8,128)(2,1)S(1)} %pad_maximum_fusion.refs_10_), channel_id=1, source_target_pairs={{0,12},{1,13},{2,14},{3,15},{4,0},{5,1},{6,2},{7,3},{8,4},{9,5},{1... | collective-permute-start | bytes 491528 | tf_op jit(solution)/shard_map/zq3/ppermute | solution.py:53
  110.5 8.4 %collective-permute-start.29 = (bf16[2,400,128]{2,1,0:T(8,128)(2,1)}, bf16[2,400,128]{2,1,0:T(8,128)(2,1)S(1)}, u32[]{:S(2)}, u32[]{:S(2)}) collective-permute-start(bf16[2,400,128]{2,1,0:T(8,128)(2,1)} %attend.1.refs_0_), channel_id=1, source_target_pairs={{0,4},{1,5},{2,6},{3,7},{4,8},{5,9},{6,10},{7,11},{8,12},{9,13},{1... | collective-permute-start | bytes 614408 | tf_op jit(solution)/shard_map/oz1/ppermute | solution.py:53
  110.5 8.3 %collective-permute-start.32 = (bf16[2,400,128]{2,1,0:T(8,128)(2,1)}, bf16[2,400,128]{2,1,0:T(8,128)(2,1)S(1)}, u32[]{:S(2)}, u32[]{:S(2)}) collective-permute-start(bf16[2,400,128]{2,1,0:T(8,128)(2,1)} %attend.1.refs_0_), channel_id=1, source_target_pairs={{0,2},{1,3},{2,0},{3,1},{4,6},{5,7},{6,4},{7,5},{8,10},{9,11},{10,... | collective-permute-start | bytes 614408 | tf_op jit(solution)/shard_map/oy0/ppermute | solution.py:53
  111.6 10.4 %collective-permute-start.31 = (bf16[2,400,128]{2,1,0:T(8,128)(2,1)}, bf16[2,400,128]{2,1,0:T(8,128)(2,1)S(1)}, u32[]{:S(2)}, u32[]{:S(2)}) collective-permute-start(bf16[2,400,128]{2,1,0:T(8,128)(2,1)} %attend.1.refs_0_), channel_id=1, source_target_pairs={{0,12},{1,13},{2,14},{3,15},{4,0},{5,1},{6,2},{7,3},{8,4},{9,5},{1... | collective-permute-start | bytes 614408 | tf_op jit(solution)/shard_map/oz3/ppermute | solution.py:53
  118.9 7.6 %collective-permute-start.30 = (bf16[2,400,128]{2,1,0:T(8,128)(2,1)S(1)}, bf16[2,400,128]{2,1,0:T(8,128)(2,1)S(1)}, u32[]{:S(2)}, u32[]{:S(2)}) collective-permute-start(bf16[2,400,128]{2,1,0:T(8,128)(2,1)S(1)} %collective-permute-done.29.refs_1_), channel_id=1, source_target_pairs={{0,4},{1,5},{2,6},{3,7},{4,8},{5,9},{6,10},{7,11},{8,12},{9,13},{1... | collective-permute-start | bytes 614408 | tf_op jit(solution)/shard_map/oz2/ppermute | solution.py:53
  118.9 9.0 %collective-permute-start.33 = (bf16[2,400,128]{2,1,0:T(8,128)(2,1)S(1)}, bf16[2,400,128]{2,1,0:T(8,128)(2,1)S(1)}, u32[]{:S(2)}, u32[]{:S(2)}) collective-permute-start(bf16[2,400,128]{2,1,0:T(8,128)(2,1)S(1)} %collective-permute-done.29.refs_1_), channel_id=1, source_target_pairs={{0,2},{1,3},{2,0},{3,1},{4,6},{5,7},{6,4},{7,5},{8,10},{9,11},{10,... | collective-permute-start | bytes 614408 | tf_op jit(solution)/shard_map/oy1/ppermute | solution.py:53
  122.0 7.8 %collective-permute-start.35 = (bf16[2,400,128]{2,1,0:T(8,128)(2,1)S(1)}, bf16[2,400,128]{2,1,0:T(8,128)(2,1)S(1)}, u32[]{:S(2)}, u32[]{:S(2)}) collective-permute-start(bf16[2,400,128]{2,1,0:T(8,128)(2,1)S(1)} %collective-permute-done.31.refs_3_), channel_id=1, source_target_pairs={{0,2},{1,3},{2,0},{3,1},{4,6},{5,7},{6,4},{7,5},{8,10},{9,11},{10,... | collective-permute-start | bytes 614408 | tf_op jit(solution)/shard_map/oy3/ppermute | solution.py:53
  126.4 5.8 %collective-permute-start.34 = (bf16[2,400,128]{2,1,0:T(8,128)(2,1)S(1)}, bf16[2,400,128]{2,1,0:T(8,128)(2,1)S(1)}, u32[]{:S(2)}, u32[]{:S(2)}) collective-permute-start(bf16[2,400,128]{2,1,0:T(8,128)(2,1)S(1)} %collective-permute-done.30.refs_2_), channel_id=1, source_target_pairs={{0,2},{1,3},{2,0},{3,1},{4,6},{5,7},{6,4},{7,5},{8,10},{9,11},{10,... | collective-permute-start | bytes 614408 | tf_op jit(solution)/shard_map/oy2/ppermute | solution.py:53
  140.2 2.0 %collective-permute-start.36 = (bf16[16,128,128]{2,1,0:T(8,128)(2,1)S(1)}, bf16[16,128,128]{2,1,0:T(8,128)(2,1)S(1)}, u32[]{:S(2)}, u32[]{:S(2)}) collective-permute-start(bf16[16,128,128]{2,1,0:T(8,128)(2,1)S(1)} %get-tuple-element.94), channel_id=1, source_target_pairs={{0,1},{1,0},{2,3},{3,2},{4,5},{5,4},{6,7},{7,6},{8,9},{9,8},{10,11... | collective-permute-start | bytes 1572872 | tf_op jit(solution)/shard_map/swap_attended/ppermute | solution.py:53
  (15 other events, 79.9 us)
